TPU v7x, 32 devices: a whole 2x2x4 slice. The times are simulated.
32 devices in a mesh: segment: 2 (over core), dp: 4 (over z), rows: 4 (over y, x).
Axes of the slice: x: 2, y: 2, z: 4, core: 2. Of those that a mesh axis runs over, the one named last changes fastest.
Arguments:
- latent: bfloat16 [8, 16, 16, 320], P('dp', 'rows'), may hold values from -6 to 6
- hint: bfloat16 [8, 16, 16, 320], P('dp', 'rows'), may hold values from -6 to 6
- decoder_in: bfloat16 [8, 16, 16, 320], P('dp', 'rows'), may hold values from -6 to 6
- target: bfloat16 [8, 16, 16, 320], P('dp', 'rows'), may hold values from -6 to 6
- first_convs: bfloat16 [2, 2, 2880, 320], P('segment', None, 'dp'), may hold values from -0.109375 to 0.109375
- second_convs: bfloat16 [2, 2880, 320], P('segment', 'dp'), may hold values from -0.109375 to 0.109375
- pointwise_weights: bfloat16 [2, 2, 320, 320], P('segment', None, 'dp'), may hold values from -0.3125 to 0.3125
Outputs:
- grad_first: float32 [921600], P(('segment', 'dp', 'rows'))
- grad_zero: float32 [102400], P(('segment', 'dp', 'rows'))
All inputs are finite; a program needn't handle non-finite values.
Results may differ from a plain program's by a relative error of at most 0.0095.
Values may be sent and summed in bfloat16 or wider, within the bound.
No kernel may reach another device: no remote copies, remote signals or barrier semaphores. Data moves between devices by JAX's collectives and lax.ppermute only.
A program may use at most 64 MiB of HBM per device.

v0:
```python
import functools
import math

import jax
import jax.numpy as jnp
from jax import lax
from jax.experimental import pallas as pl
from jax.experimental.pallas import tpu as pltpu
from jax.sharding import PartitionSpec as P

BF16 = jnp.bfloat16
F32 = jnp.float32


def slope(value):
    logistic = 1.0 / (1.0 + jnp.exp(-value))
    return logistic * (1.0 + value * (1.0 - logistic))


def silu(value):
    return value / (1.0 + jnp.exp(-value))


def mm(left, right):
    return jnp.dot(left, right, preferred_element_type=F32)


def spread(wide, sample, values, width):
    cells, channels = values.shape
    height = cells // width
    full = values.astype(F32)
    column = lax.broadcasted_iota(jnp.int32, (cells, channels), 0) % width
    before = jnp.where(column == 0, 0.0, pltpu.roll(full, 1, 0)).astype(BF16)
    after = jnp.where(column == width - 1, 0.0, pltpu.roll(full, cells - 1, 0)).astype(BF16)
    row = jnp.concatenate([before, values, after], axis=1)
    edge = jnp.zeros((width, 3 * channels), BF16)
    wide[sample, 0:width] = edge
    wide[sample, width : width + cells] = row
    wide[sample, width + cells : 2 * width + cells] = edge


def conv(wide, sample, weight, width):
    cells = wide.shape[1] - 2 * width
    depth = wide.shape[2]
    total = None
    for a in range(3):
        part = mm(wide[sample, a * width : a * width + cells], weight[a * depth : (a + 1) * depth])
        total = part if total is None else total + part
    return total


def flip(weight, back):
    channels = weight.shape[1]
    for tap in range(9):
        block = weight[tap * channels : (tap + 1) * channels]
        back[(8 - tap) * channels : (9 - tap) * channels] = block.T


def load(copies, sem):
    handles = [pltpu.make_async_copy(src, dst, sem.at[k]) for k, (src, dst) in enumerate(copies)]
    for handle in handles:
        handle.start()
    for handle in handles:
        handle.wait()


def first_kernel(dims, seg, pair, kernels, points, act, base, held, wide, pre, extra):
    samples, parts, step, width, channels = dims
    cells = parts * step * width

    def whole(which, sample):
        return jnp.concatenate(
            [
                pair[part, which, sample].reshape(step * width, channels)
                for part in range(parts)
            ],
            axis=0,
        )

    @pl.when(seg[0] == 0)
    def _():
        for n in range(samples):
            latent = whole(0, n)
            spread(wide, n, latent, width)
            act[0, n] = silu(conv(wide, n, kernels.at[0], width)).astype(BF16)
            act[1, n] = latent
            mixed = latent.astype(F32) + mm(whole(1, n), points[0])
            mixed = mixed.astype(BF16)
            base[n] = mixed
            spread(wide, n, mixed, width)
            out = conv(wide, n, kernels.at[1], width)
            pre[n] = out
            held[n] = silu(out).astype(BF16)

    @pl.when(seg[0] != 0)
    def _():
        for n in range(samples):
            given = whole(0, n)
            base[n] = whole(1, n)
            spread(wide, n, given, width)
            pre[n] = conv(wide, n, kernels.at[1], width)
            extra[n] = mm(given, points[0])


def second_kernel(dims, seg, sent, held, base, kernels, second, points, proj, out, skip, wide):
    samples, parts, step, width, channels = dims

    @pl.when(seg[0] == 0)
    def _():
        for n in range(samples):
            spread(wide, n, held[n], width)
            value = base[n].astype(F32) + conv(wide, n, second, width)
            value = value.astype(BF16)
            out[n] = value
            proj[n] = mm(value, points[1]).astype(BF16)

    @pl.when(seg[0] != 0)
    def _():
        for n in range(samples):
            spread(wide, n, sent[0, n], width)
            skip[n] = sent[1, n].astype(F32) + conv(wide, n, kernels.at[0], width)


def third_kernel(dims, scale, seg, proj, skip, pre, extra, target, second, points, grad, wide, back):
    samples, parts, step, width, channels = dims

    @pl.when(seg[0] != 0)
    def _():
        flip(second, back)
        for n in range(samples):
            value = (skip[n] + proj[n].astype(F32)).astype(BF16)
            spread(wide, n, value, width)
            before = pre[n] + conv(wide, n, second, width)
            output = silu(before) + extra[n] + mm(value, points[1])
            error = (output - target[n].astype(F32)) * scale
            spread(wide, n, (error * slope(before)).astype(BF16), width)
            total = conv(wide, n, back, width) + mm(error.astype(BF16), points[1].T)
            grad[n] = total.astype(BF16)


def fourth_kernel(dims, seg, grad, base, out, pre, second, points, first, zero, wide, back):
    samples, parts, step, width, channels = dims
    cells = parts * step * width

    @pl.when(seg[0] == 0)
    def _():
        flip(second, back)
        for n in range(samples):
            given = grad[n]
            partial = lax.dot_general(
                out[n], given, (((0,), (0,)), ((), ())), preferred_element_type=F32
            )
            zero[...] = partial if n == 0 else zero[...] + partial
            spread(wide, n, mm(given, points[1].T).astype(BF16), width)
            cot = (conv(wide, n, back, width) * slope(pre[n])).astype(BF16)
            spread(wide, n, base[n], width)
            for a in range(3):
                partial = lax.dot_general(
                    wide[n, a * width : a * width + cells],
                    cot,
                    (((0,), (0,)), ((), ())),
                    preferred_element_type=F32,
                )
                rows = slice(3 * a * channels, 3 * (a + 1) * channels)
                first[rows] = partial if n == 0 else first[rows] + partial

    @pl.when(seg[0] != 0)
    def _():
        first[...] = jnp.zeros(first.shape, F32)
        zero[...] = jnp.zeros(zero.shape, F32)


def call(body, outs, scratch, *args, limit=12, work=0):
    vmem = pl.BlockSpec(memory_space=pltpu.VMEM)
    smem = pl.BlockSpec(memory_space=pltpu.SMEM)
    return pl.pallas_call(
        body,
        out_shape=[jax.ShapeDtypeStruct(shape, dtype) for shape, dtype in outs],
        in_specs=[smem] + [vmem] * (len(args) - 1),
        out_specs=[vmem] * len(outs),
        scratch_shapes=[pltpu.VMEM(shape, dtype) for shape, dtype in scratch],
        compiler_params=pltpu.CompilerParams(vmem_limit_bytes=limit * 1024 * 1024),
        cost_estimate=pl.CostEstimate(flops=work, bytes_accessed=0, transcendentals=0),
    )(*args)


def gathered(block, cut):
    depth, width = block.shape
    parts = lax.axis_size("rows")
    if depth % cut:
        return lax.all_gather(block, "dp", axis=0, tiled=True)
    units = -(-(depth // cut) // parts)
    size = units * cut
    if size * (parts - 1) >= depth:
        return lax.all_gather(block, "dp", axis=0, tiled=True)
    start = jnp.minimum(lax.axis_index("rows") * size, depth - size)
    piece = lax.dynamic_slice_in_dim(block, start, size, 0)
    whole = lax.all_gather(piece, ("dp", "rows"), axis=0, tiled=True)
    if size * parts == depth:
        return whole
    count = lax.axis_size("dp")
    whole = whole.reshape(count, parts, size, width)
    body = whole[:, : parts - 1].reshape(count, (parts - 1) * size, width)
    tail = whole[:, parts - 1, parts * size - depth :]
    return jnp.concatenate([body, tail], axis=1).reshape(count * depth, width)


def role(ids, segment, row):
    return jnp.logical_and(ids[0] == segment, ids[2] == row)


def view(ref, n, cells, channels):
    left = n % 2 * channels
    return ref.at[n // 2 * cells : (n // 2 + 1) * cells, left : left + channels]


def halves(ref):
    rows = ref.shape[0] // 2
    return ref.at[:rows], ref.at[rows:]


def put(piece, base, kern, maps, map_base):
    half, channels = piece.shape[0], kern.shape[1]
    taps, rows = kern.shape[0] // 4, maps.shape[0] // 4
    kern[pl.ds(base, half)] = piece[:, :channels]
    kern[pl.ds(pl.multiple_of(base + half, 16), taps - half)] = piece[: taps - half, channels:]
    maps[pl.ds(map_base, rows)] = piece[taps - half :, channels:]


def place(ids, pieces, kern, maps):
    taps, rows = kern.shape[0] // 4, maps.shape[0] // 4
    inner = jnp.logical_or(ids[1] == 1, ids[1] == 2)
    for spot, (k, piece) in enumerate(zip((0, 2, 3, 1, 3), pieces)):
        group = lax.bitwise_xor(ids[1], k)
        base = pl.multiple_of(group * taps, 16)
        map_base = pl.multiple_of(group * rows, 16)
        if k < 3 or len(pieces) == 4:
            put(piece, base, kern, maps, map_base)
        else:

            @pl.when(inner if spot == 2 else jnp.logical_not(inner))
            def _(piece=piece, base=base, map_base=map_base):
                put(piece, base, kern, maps, map_base)


def early_kernel(width, ids, *refs):
    mine, pieces = refs[:4], refs[4:8]
    images, sent, mixed, bend, kern, maps, wide = refs[8:]
    samples, whole, channels = images.shape[1:]
    act, same = halves(sent)
    for k, part in enumerate(mine):
        cells = part.shape[0] // samples
        spot = pl.multiple_of(lax.bitwise_xor(ids[2], k) * cells, 16)
        for which in range(2):
            for n in range(samples):
                images[which, n, pl.ds(spot, cells)] = part[
                    n * cells : (n + 1) * cells, which * channels : (which + 1) * channels
                ]

    @pl.when(role(ids, 0, 0))
    def _():
        place(ids, pieces, kern, maps)
        for n in range(samples):
            value = (images[0, n].astype(F32) + mm(images[1, n], maps[...])).astype(BF16)
            view(mixed, n, whole, channels)[...] = value
            view(same, n, whole, channels)[...] = value
            spread(wide, n, value, width)
            out = conv(wide, n, kern, width)
            view(act, n, whole, channels)[...] = silu(out).astype(BF16)
            view(bend, n, whole, channels)[...] = slope(out).astype(BF16)

    @pl.when(role(ids, 0, 2))
    def _():
        place(ids, pieces, kern, maps)
        for n in range(samples):
            latent = images[0, n]
            view(same, n, whole, channels)[...] = latent
            spread(wide, n, latent, width)
            view(act, n, whole, channels)[...] = silu(conv(wide, n, kern, width)).astype(BF16)


def given_kernel(width, ids, images, *refs):
    pieces = refs[:4]
    sides, kern, maps, wide = refs[4:]
    samples, cells, channels = images.shape[1:]
    given, extra = halves(sides)

    @pl.when(role(ids, 1, 3))
    def _():
        place(ids, pieces, kern, maps)
        for n in range(samples):
            value = images[0, n]
            spread(wide, n, value, width)
            view(given, n, cells, channels)[...] = conv(wide, n, kern, width).astype(BF16)
            view(extra, n, cells, channels)[...] = mm(value, maps[...]).astype(BF16)


def rows_at(ref, start, extra, count):
    first = pl.multiple_of(start + extra // 8 * 8, 8)
    return ref[pl.ds(first, count + 8)][extra % 8 : extra % 8 + count]


def columns_kernel(width, groups, ids, own, near, below, across, chosen, base, wide, turned):
    @pl.when(ids[0] == 0)
    def _():
        for row, source in enumerate((own, halves(near)[1], below, across)):

            @pl.when(ids[2] == row)
            def _(source=source):
                base[...] = source[...]

        samples, channels = wide.shape[0], wide.shape[2] // 3
        cells = wide.shape[1] - 2 * width
        for n in range(samples):
            spread(wide, n, view(base, n, cells, channels)[...], width)
            for a in range(3):
                turned[
                    3 * a * channels : 3 * (a + 1) * channels, n * cells : (n + 1) * cells
                ] = wide[n, a * width : a * width + cells].astype(F32).T
        block = 9 * channels // (2 * groups)
        share = block // 4
        for row in range(4):

            @pl.when(ids[2] == row)
            def _(row=row):
                for k in range(4):
                    for half in range(2):
                        start = (half * groups + lax.bitwise_xor(ids[1], k)) * block
                        chosen[k, half] = rows_at(
                            turned, start, share * row, chosen.shape[2]
                        ).astype(BF16)


def skip_kernel(width, ids, near, *refs):
    pieces = refs[:4]
    skip, kern, maps, wide = refs[4:]
    samples, channels = wide.shape[0], wide.shape[2] // 3
    cells = wide.shape[1] - 2 * width
    near, latent = halves(near)

    @pl.when(role(ids, 1, 2))
    def _():
        place(ids, pieces, kern, maps)
        for n in range(samples):
            spread(wide, n, view(near, n, cells, channels)[...], width)
            total = view(latent, n, cells, channels)[...].astype(F32) + conv(wide, n, kern, width)
            view(skip, n, cells, channels)[...] = total.astype(BF16)


def layout_kernel(ids, sides, *refs):
    pieces = refs[:5]
    kern, back, maps = refs[5:]

    @pl.when(ids[2] == 1)
    def _():
        place(ids, pieces, kern, maps)

        @pl.when(ids[0] == 1)
        def _():
            flip(kern, back)


def middle_kernel(width, ids, near, kern, maps, out, proj, wide):
    samples, channels = wide.shape[0], wide.shape[2] // 3
    cells = wide.shape[1] - 2 * width
    near, mixed = halves(near)

    @pl.when(role(ids, 0, 1))
    def _():
        for n in range(samples):
            spread(wide, n, view(near, n, cells, channels)[...], width)
            value = view(mixed, n, cells, channels)[...].astype(F32)
            value = (value + conv(wide, n, kern, width)).astype(BF16)
            out[n] = value
            view(proj, n, cells, channels)[...] = mm(value, maps[...]).astype(BF16)


def decoder_kernel(
    width, scale, ids, proj, skip, sides, images, kern, back, maps, grad, turned, wide
):
    samples, cells, channels = images.shape[1:]
    given, extra = halves(sides)

    @pl.when(role(ids, 0, 1))
    def _():
        flip(kern, turned)

    @pl.when(role(ids, 1, 1))
    def _():
        for n in range(samples):

            def part(ref):
                return view(ref, n, cells, channels)[...].astype(F32)

            value = (part(skip) + part(proj)).astype(BF16)
            spread(wide, n, value, width)
            before = part(given) + conv(wide, n, kern, width)
            output = silu(before) + part(extra) + mm(value, maps[...])
            error = (output - images[1, n].astype(F32)) * scale
            spread(wide, n, (error * slope(before)).astype(BF16), width)
            total = conv(wide, n, back, width) + mm(error.astype(BF16), maps[...].T)
            view(grad, n, cells, channels)[...] = total.astype(BF16)


def control_kernel(width, groups, ids, grad, bend, out, turned, maps, parcel, zero, wide):
    @pl.when(role(ids, 0, 1))
    def _():
        samples, cells, channels = out.shape
        for n in range(samples):
            given = view(grad, n, cells, channels)[...]
            partial = lax.dot_general(
                out[n], given, (((0,), (0,)), ((), ())), preferred_element_type=F32
            )
            rows = slice(0, channels)
            zero[rows] = partial if n == 0 else zero[rows] + partial
            spread(wide, n, mm(given, maps[...].T).astype(BF16), width)
            bent = view(bend, n, cells, channels)[...].astype(F32)
            cot = (conv(wide, n, turned, width) * bent).astype(BF16)
            for k in range(4):
                view(parcel.at[k], n, cells, channels)[...] = cot
        block = channels // (2 * groups)
        share = block // 4
        tall = 16
        for k in range(4):
            for other in range(4):
                for half in range(2):
                    start = (half * groups + lax.bitwise_xor(ids[1], other)) * block
                    spot = samples // 2 * cells + other * tall
                    parcel[
                        k, spot : spot + tall, half * channels : (half + 1) * channels
                    ] = rows_at(zero, start, share * (1 ^ k), tall).astype(BF16)


def gradient_kernel(shares, ids, chosen, parcel, first, second, third, kept, sent, taken, flat):
    @pl.when(ids[0] == 0)
    def _():
        for row, source in ((0, first), (1, parcel.at[0]), (2, third), (3, second)):

            @pl.when(ids[2] == row)
            def _(source=source):
                taken[...] = source[...]

        tall, depth = chosen.shape[2], chosen.shape[3]
        channels = flat.shape[1]
        small = 16
        body = depth // 2
        for half in range(2):
            flat[half * body : (half + 1) * body] = taken[
                :body, half * channels : (half + 1) * channels
            ]
        rows = kept.shape[1]
        for k in range(4):
            group = lax.bitwise_xor(ids[1], k)
            spot = body + k * small
            for half, target in enumerate((kept, sent)):
                lanes = slice(half * channels, (half + 1) * channels)
                part = [
                    mm(chosen[k, half], flat[...])[: shares[0]],
                    taken[spot : spot + small, lanes].astype(F32)[: shares[1]],
                    jnp.zeros((2 * rows - sum(shares), channels), F32),
                ]
                value = jnp.concatenate(part, axis=0).astype(target.dtype)
                target[group, :, :channels] = value[:rows]
                target[group, :, channels:] = value[rows:]


def us(time):
    return int(time * 1.15e9)


def hop(values, sizes, moves):
    segments, groups, parts = sizes

    def flat(place):
        return (place[0] * groups + place[1]) * parts + place[2]

    pairs = []
    for s in range(segments):
        for d in range(groups):
            for r in range(parts):
                target = moves(s, d, r)
                if target is not None:
                    pairs.append((flat((s, d, r)), flat(target)))
    return lax.ppermute(values, ("segment", "dp", "rows"), pairs)


def fits(latent, first_convs, pointwise_weights):
    samples, step, width, channels = latent.shape
    taps, maps = first_convs.shape[2], pointwise_weights.shape[2]
    groups, parts = lax.axis_size("dp"), lax.axis_size("rows")
    half = (taps + maps) // 2
    return (
        lax.axis_size("segment") == 2
        and groups == 4
        and parts == 4
        and samples == 2
        and width % 16 == 0
        and taps % 16 == 0
        and maps % 16 == 0
        and half % 16 == 0
        and half <= taps
        and channels % (2 * groups * parts) == 0
        and channels // (2 * groups * parts) <= 16
        and channels // (2 * groups) % 8 == 0
    )


def by_roles(latent, hint, decoder_in, target, first_convs, second_convs, pointwise_weights):
    samples, step, width, channels = latent.shape
    parts, groups = lax.axis_size("rows"), lax.axis_size("dp")
    cells = parts * step * width
    segment, group, row = (lax.axis_index(axis) for axis in ("segment", "dp", "rows"))
    ids = jnp.stack([segment, group, row]).astype(jnp.int32)
    scale = 1.0 / math.sqrt(samples * groups * cells)
    sizes = (lax.axis_size("segment"), groups, parts)
    taps, rows = first_convs.shape[2], pointwise_weights.shape[2]
    plane = (samples, cells, channels)
    pair = (samples // 2 * cells, 2 * channels)
    wide = ((samples, cells + 2 * width, 3 * channels), BF16)
    kern = ((9 * channels, channels), BF16)
    maps = ((channels, channels), BF16)

    kernel = lax.dynamic_index_in_dim(
        first_convs[0], (row % 3 == 0).astype(jnp.int32), 0, keepdims=False
    )
    kernel = jnp.where(row == 1, second_convs[0], kernel)
    half = (taps + rows) // 2

    def pack(kernel, point):
        bundle = jnp.concatenate([kernel, point], axis=0)
        return jnp.concatenate([bundle[:half], bundle[half:]], axis=1)

    packed = pack(kernel, jnp.where(row == 1, pointwise_weights[0, 1], pointwise_weights[0, 0]))
    soon, late, again = ((0, 0), (0, 2), (1, 3)), ((0, 1), (1, 1)), ((1, 2),)
    homes = soon + late

    def across_groups(values, k, some):
        return hop(values, sizes, lambda s, d, r: (s, d ^ k, r) if (s, r) in some else None)

    two, one = (across_groups(packed, k, homes) for k in (2, 1))
    mine = jnp.concatenate(
        [
            jnp.where(segment == 0, a, b).reshape(-1, channels)
            for a, b in ((latent, decoder_in), (hint, target))
        ],
        axis=1,
    )
    others = [hop(mine, sizes, lambda s, d, r: (s, d, r ^ k)) for k in (1, 2, 3)]

    early = (packed, two, across_groups(packed, 3, soon), one)
    tied, *others = lax.optimization_barrier((packed, *others))
    later = (tied, *(across_groups(tied, k, again) for k in (2, 3, 1)))
    two, one, direct = lax.optimization_barrier((two, one, packed))
    ends = [
        hop(
            values,
            sizes,
            lambda s, d, r: (s, d ^ k, r) if (s, r) in late and d in (1, 2) else None,
        )
        for k, values in ((3, direct), (1, two))
    ]
    last = (direct, two, ends[0], one, ends[1])

    def one_hop(values, *moves):
        table = dict(moves)

        def move(s, d, r):
            target = table.get((s, r))
            return None if target is None else (target[0], d, target[1])

        return hop(values, sizes, move)

    images, sent, mixed, bend = call(
        functools.partial(early_kernel, width),
        [
            ((2,) + plane, BF16),
            ((2 * pair[0], pair[1]), BF16),
            (pair, BF16),
            (pair, BF16),
        ],
        [kern, maps, wide],
        ids,
        mine,
        *others,
        *early,
        work=us(4.4),
    )
    near = one_hop(sent, ((0, 0), (0, 1)))
    encoded = one_hop(sent, ((0, 2), (1, 2)))
    below = one_hop(mixed, ((0, 0), (0, 2)))
    across = one_hop(mixed, ((0, 0), (0, 3)))
    bend = one_hop(bend, ((0, 0), (0, 1)))
    (sides,) = call(
        functools.partial(given_kernel, width),
        [((2 * pair[0], pair[1]), BF16)],
        [kern, maps, wide],
        ids,
        images,
        *early,
        work=us(3.5),
    )
    kernel, back, point = call(
        layout_kernel, [kern, kern, maps], [], ids, sides, *last, work=us(2)
    )
    sides = one_hop(sides, ((1, 3), (1, 1)))
    kernel, point, near = lax.optimization_barrier((kernel, point, near))
    out, proj = call(
        functools.partial(middle_kernel, width),
        [(plane, BF16), (pair, BF16)],
        [wide],
        ids,
        near,
        kernel,
        point,
        work=us(3),
    )
    proj, encoded = lax.optimization_barrier((proj, encoded))
    (skip,) = call(
        functools.partial(skip_kernel, width),
        [(pair, BF16)],
        [kern, maps, wide],
        ids,
        encoded,
        *later,
        work=us(3.5),
    )
    skip = one_hop(skip, ((1, 2), (1, 1)))
    moved = one_hop(proj, ((0, 1), (1, 1)))
    grad, turned = call(
        functools.partial(decoder_kernel, width, scale),
        [(pair, BF16), kern],
        [wide],
        ids,
        moved,
        skip,
        sides,
        images,
        kernel,
        back,
        point,
        work=us(6),
    )
    tall = -(-(9 * channels // (2 * groups * parts)) // 16) * 16
    (chosen,) = call(
        functools.partial(columns_kernel, width, groups),
        [((4, 2, tall, samples * cells), BF16)],
        [(pair, BF16), wide, ((9 * channels + 24, samples * cells), F32)],
        ids,
        mixed,
        near,
        below,
        across,
        work=us(2),
    )
    grad = one_hop(grad, ((1, 1), (0, 1)))
    grad, chosen = lax.optimization_barrier((grad, chosen))
    body = (pair[0] + 4 * 16, pair[1])
    (parcel,) = call(
        functools.partial(control_kernel, width, groups),
        [((4,) + body, BF16)],
        [((channels + 24, channels), F32), wide],
        ids,
        grad,
        bend,
        out,
        turned,
        point,
        work=us(3.6),
    )
    spread_out = [one_hop(parcel[k], ((0, 1), (0, 1 ^ k))) for k in (1, 2, 3)]
    count = 2 * groups * parts
    shares = (9 * channels // count, channels // count)
    block = (-(-sum(shares) // 16) * 8, 2 * channels)
    kept, sent = call(
        functools.partial(gradient_kernel, shares),
        [((groups,) + block, BF16)] * 2,
        [(body, BF16), ((samples * cells, channels), BF16)],
        ids,
        chosen,
        parcel,
        *spread_out,
    )
    sent = one_hop(sent, *(((0, r), (1, r)) for r in range(parts)))
    sent = jnp.where(segment == 0, kept, sent)
    total = jnp.sum(lax.all_to_all(sent, "dp", 0, 0).astype(F32), axis=0)
    result = jnp.concatenate([total[:, :channels], total[:, channels:]], axis=0)
    flat = result[: sum(shares)].reshape(-1)
    return (flat[: shares[0] * channels], flat[shares[0] * channels :])


def per_device(latent, hint, decoder_in, target, first_convs, second_convs, pointwise_weights):
    if fits(latent, first_convs, pointwise_weights):
        return by_roles(
            latent, hint, decoder_in, target, first_convs, second_convs, pointwise_weights
        )
    samples, step, width, channels = latent.shape
    parts, groups = lax.axis_size("rows"), lax.axis_size("dp")
    cells = parts * step * width
    segment = lax.axis_index("segment")
    seg = segment.reshape(1).astype(jnp.int32)
    scale = 1.0 / math.sqrt(samples * groups * cells)
    dims = (samples, parts, step, width, channels)

    mine = jnp.stack(
        [jnp.where(segment == 0, latent, decoder_in), jnp.where(segment == 0, hint, target)]
    )
    pair = lax.all_gather(mine, "rows")

    taps = first_convs.shape[2]
    maps = pointwise_weights.shape[2]
    stacked = jnp.concatenate(
        [first_convs.reshape(2 * taps, channels), pointwise_weights.reshape(2 * maps, channels)],
        axis=0,
    )
    both = gathered(stacked, 16).reshape(groups, 2 * (taps + maps), channels)
    kernels = jnp.stack(
        [both[:, k * taps : (k + 1) * taps].reshape(groups * taps, channels) for k in range(2)]
    )
    points = jnp.stack(
        [
            both[:, 2 * taps + k * maps : 2 * taps + (k + 1) * maps].reshape(channels, channels)
            for k in range(2)
        ]
    )
    second = gathered(second_convs.reshape(taps, channels), 16)

    plane = (samples, cells, channels)
    wide = ((samples, cells + 2 * width, 3 * channels), BF16)
    back = ((9 * channels, channels), BF16)
    act, base, held, pre, extra = call(
        lambda seg, pair, kernels, points, act, base, held, pre, extra, wide: first_kernel(
            dims, seg, pair, kernels, points, act, base, held, wide, pre, extra
        ),
        [((2,) + plane, BF16), (plane, BF16), (plane, BF16), (plane, F32), (plane, F32)],
        [wide],
        seg,
        pair,
        kernels,
        points,
    )
    sent = lax.ppermute(act, "segment", [(0, 1)])
    proj, out, skip = call(
        functools.partial(second_kernel, dims),
        [(plane, BF16), (plane, BF16), (plane, F32)],
        [wide],
        seg,
        sent,
        held,
        base,
        kernels,
        second,
        points,
    )
    proj = lax.ppermute(proj, "segment", [(0, 1)])
    (grad,) = call(
        functools.partial(third_kernel, dims, scale),
        [(plane, BF16)],
        [wide, back],
        seg,
        proj,
        skip,
        pre,
        extra,
        base,
        second,
        points,
    )
    grad = lax.ppermute(grad, "segment", [(1, 0)])
    first, zero = call(
        functools.partial(fourth_kernel, dims),
        [((9 * channels, channels), F32), ((channels, channels), F32)],
        [wide, back],
        seg,
        grad,
        base,
        out,
        pre,
        second,
        points,
    )
    once = lax.axis_index("rows") == 0
    axes = ("segment", "dp", "rows")
    return tuple(
        lax.psum_scatter(
            jnp.where(once, value, 0.0).reshape(-1), axes, scatter_dimension=0, tiled=True
        )
        for value in (first, zero)
    )


def solution(mesh):
    spread_out = P("dp", "rows", None, None)
    placed = (
        spread_out,
        spread_out,
        spread_out,
        spread_out,
        P("segment", None, "dp", None),
        P("segment", "dp", None),
        P("segment", None, "dp", None),
    )
    return jax.shard_map(
        per_device,
        mesh=mesh,
        in_specs=placed,
        out_specs=(P(("segment", "dp", "rows")), P(("segment", "dp", "rows"))),
        check_vma=False,
    )
```

profile of v0, /device:TPU:4, one launch (start us, length us, event | category | flops | bytes accessed | tf_op | source)
XLA Modules:
  0.0 107.8 jit_solution(1729999609509836541)
XLA Ops:
  0.7 1.2 %copy-done = bf16[1,2,720,320]{2,3,1,0:T(8,128)(2,1)S(1)} copy-done((bf16[1,2,720,320]{2,3,1,0:T(8,128)(2,1)S(1)}, bf16[1,2,720,320]{2,3,1,0:T(8,128)(2,1)}, u32[]{:S(2)}) %copy-start) | copy-done | bytes 921624
  3.0 4.5 %collective-permute-start.3 = (bf16[400,640]{1,0:T(8,128)(2,1)S(1)}, bf16[400,640]{1,0:T(8,128)(2,1)S(1)}, u32[]{:S(2)}, u32[]{:S(2)}) collective-permute-start(bf16[400,640]{1,0:T(8,128)(2,1)S(1)} %fusion.refs_4_.refs_0_), channel_id=1, source_target_pairs={{0,8},{1,9},{2,10},{4,12},{5,13},{6,14},{8,0},{9,1},{10,2},{12,4},... | collective-permute-start | bytes 1536008 | tf_op jit(solution)/shard_map/ppermute | solution.py:484
  7.5 3.5 %collective-permute-start.5 = (bf16[400,640]{1,0:T(8,128)(2,1)S(1)}, bf16[400,640]{1,0:T(8,128)(2,1)S(1)}, u32[]{:S(2)}, u32[]{:S(2)}) collective-permute-start(bf16[400,640]{1,0:T(8,128)(2,1)S(1)} %fusion.refs_4_.refs_0_), channel_id=1, source_target_pairs={{0,4},{1,5},{2,6},{4,0},{5,1},{6,2},{8,12},{9,13},{10,14},{12,8},{... | collective-permute-start | bytes 1536008 | tf_op jit(solution)/shard_map/ppermute | solution.py:484
  11.0 2.1 %collective-permute-start.4 = (bf16[400,640]{1,0:T(8,128)(2,1)S(1)}, bf16[400,640]{1,0:T(8,128)(2,1)S(1)}, u32[]{:S(2)}, u32[]{:S(2)}) collective-permute-start(bf16[400,640]{1,0:T(8,128)(2,1)S(1)} %fusion.refs_4_.refs_0_), channel_id=1, source_target_pairs={{0,12},{2,14},{4,8},{6,10},{8,4},{10,6},{12,0},{14,2},{19,31},{23,... | collective-permute-start | bytes 1536008 | tf_op jit(solution)/shard_map/ppermute | solution.py:484
  13.9 5.2 %collective-permute-done.refs_1_ = bf16[128,640]{1,0:T(8,128)(2,1)S(1)} collective-permute-done((bf16[128,640]{1,0:T(8,128)(2,1)S(1)}, bf16[128,640]{1,0:T(8,128)(2,1)S(1)}, u32[]{:S(2)}, u32[]{:S(2)}) %collective-permute-start) | collective-permute-done | bytes 163872 | tf_op jit(solution)/shard_map/ppermute | solution.py:484
  19.7 0.7 collective-permute-done.1.refs_2_
  20.4 5.1 %collective-permute-done.2.refs_3_ = bf16[128,640]{1,0:T(8,128)(2,1)} collective-permute-done((bf16[128,640]{1,0:T(8,128)(2,1)S(1)}, bf16[128,640]{1,0:T(8,128)(2,1)}, u32[]{:S(2)}, u32[]{:S(2)}) %collective-permute-start.2) | collective-permute-done | bytes 163872 | tf_op jit(solution)/shard_map/ppermute | solution.py:484
  25.5 2.8 %collective-permute-done.5.refs_7_.refs_3_ = bf16[400,640]{1,0:T(8,128)(2,1)S(1)} collective-permute-done((bf16[400,640]{1,0:T(8,128)(2,1)S(1)}, bf16[400,640]{1,0:T(8,128)(2,1)S(1)}, u32[]{:S(2)}, u32[]{:S(2)}) %collective-permute-start.5) | collective-permute-done | bytes 512032 | tf_op jit(solution)/shard_map/ppermute | solution.py:484
  28.3 0.7 collective-permute-start.6
  29.0 0.7 collective-permute-start.7
  29.7 3.6 %shard_map.86 = (bf16[2,2,256,320]{3,2,1,0:T(8,128)(2,1)S(1)}, bf16[512,640]{1,0:T(8,128)(2,1)S(1)}, bf16[256,640]{1,0:T(8,128)(2,1)S(1)}, bf16[256,640]{1,0:T(8,128)(2,1)S(1)}) custom-call(s32[3]{0:T(128)S(1)} %pad_add_fusion.ids, bf16[128,640]{1,0:T(8,128)(2,1)S(1)} %pad_maximum_fusion.1.refs_0_, bf16[128,640]{1,0:T(8,128)(2,1)S(1)} %collective-permute-done.refs_1_, ...), custom_call_target="tpu_custom_call" | custom-call | flops 5059999744 | tf_op jit(solution)/shard_map/pallas_call | solution.py:176
  33.3 0.7 collective-permute-start.8
  34.0 0.7 collective-permute-start.11
  34.7 1.3 %collective-permute-start.9 = (bf16[512,640]{1,0:T(8,128)(2,1)S(1)}, bf16[512,640]{1,0:T(8,128)(2,1)S(1)}, u32[]{:S(2)}, u32[]{:S(2)}) collective-permute-start(bf16[512,640]{1,0:T(8,128)(2,1)S(1)} %get-tuple-element.38), channel_id=1, source_target_pairs={{2,18},{6,22},{10,26},{14,30}} | collective-permute-start | bytes 1966088 | tf_op jit(solution)/shard_map/ppermute | solution.py:484
  36.6 0.7 collective-permute-start.12
  37.4 0.7 collective-permute-start.13
  38.6 0.7 collective-permute-start.15
  39.3 0.7 shard_map.89
  40.7 0.7 collective-permute-start.14
  41.4 0.7 collective-permute-start.10
  42.1 1.3 %collective-permute-start.17 = (bf16[256,640]{1,0:T(8,128)(2,1)S(1)}, bf16[256,640]{1,0:T(8,128)(2,1)S(1)}, u32[]{:S(2)}, u32[]{:S(2)}) collective-permute-start(bf16[256,640]{1,0:T(8,128)(2,1)S(1)} %get-tuple-element.48.own), channel_id=1, source_target_pairs={{0,2},{4,6},{8,10},{12,14}} | collective-permute-start | bytes 983048 | tf_op jit(solution)/shard_map/ppermute | solution.py:484
  46.0 11.2 %collective-permute-done.17.below = bf16[256,640]{1,0:T(8,128)(2,1)S(1)} collective-permute-done((bf16[256,640]{1,0:T(8,128)(2,1)S(1)}, bf16[256,640]{1,0:T(8,128)(2,1)S(1)}, u32[]{:S(2)}, u32[]{:S(2)}) %collective-permute-start.17) | collective-permute-done | bytes 327712 | tf_op jit(solution)/shard_map/ppermute | solution.py:484
  57.2 2.1 %shard_map.92.chosen = bf16[4,2,96,512]{3,2,1,0:T(8,128)(2,1)S(1)} custom-call(s32[3]{0:T(128)S(1)} %pad_add_fusion.ids, bf16[256,640]{1,0:T(8,128)(2,1)S(1)} %get-tuple-element.48.own, bf16[512,640]{1,0:T(8,128)(2,1)S(1)} %collective-permute-done.8.near, bf16[256,640]{1,0:T(8,128)(2,1)S(1)} %collective-permute-done.17.below, ...), custom_call_target="tpu_custom_call" | custom-call | flops 2300000000 | tf_op jit(solution)/shard_map/pallas_call | solution.py:176
  60.1 0.7 collective-permute-start.20
  60.8 0.7 collective-permute-start.21
  61.5 1.3 %collective-permute-start.22 = (bf16[320,640]{1,0:T(8,128)(2,1)S(1)}, bf16[320,640]{1,0:T(8,128)(2,1)S(1)}, u32[]{:S(2)}, u32[]{:S(2)}) collective-permute-start(bf16[320,640]{1,0:T(8,128)(2,1)S(1)} %get-tuple-element.56), channel_id=1, source_target_pairs={{1,2},{5,6},{9,10},{13,14}} | collective-permute-start | bytes 1228808 | tf_op jit(solution)/shard_map/ppermute | solution.py:484
  62.8 25.7 %collective-permute-done.22.third = bf16[320,640]{1,0:T(8,128)(2,1)S(1)} collective-permute-done((bf16[320,640]{1,0:T(8,128)(2,1)S(1)}, bf16[320,640]{1,0:T(8,128)(2,1)S(1)}, u32[]{:S(2)}, u32[]{:S(2)}) %collective-permute-start.22) | collective-permute-done | bytes 409632 | tf_op jit(solution)/shard_map/ppermute | solution.py:484
  88.5 1.5 %shard_map.94 = (bf16[4,56,640]{2,1,0:T(8,128)(2,1)S(1)}, bf16[4,56,640]{2,1,0:T(8,128)(2,1)S(1)}) custom-call(s32[3]{0:T(128)S(1)} %pad_add_fusion.ids, bf16[4,2,96,512]{3,2,1,0:T(8,128)(2,1)S(1)} %shard_map.92.chosen, bf16[4,320,640]{2,1,0:T(8,128)(2,1)S(1)} %shard_map.93.parcel, bf16[320,640]{1,0:T(8,128)(2,1)S(1)} %collective-permute-done.20.first, ...), custom_call_target="tpu_custom_call" | custom-call | tf_op jit(solution)/shard_map/pallas_call | solution.py:176
  90.0 1.3 %collective-permute-start.23 = (bf16[4,56,640]{2,1,0:T(8,128)(2,1)S(1)}, bf16[4,56,640]{2,1,0:T(8,128)(2,1)S(1)}, u32[]{:S(2)}, u32[]{:S(2)}) collective-permute-start(bf16[4,56,640]{2,1,0:T(8,128)(2,1)S(1)} %get-tuple-element.55), channel_id=1, source_target_pairs={{0,16},{1,17},{2,18},{3,19},{4,20},{5,21},{6,22},{7,23},{8,24},{9,... | collective-permute-start | bytes 860168 | tf_op jit(solution)/shard_map/ppermute | solution.py:484
  91.3 1.2 %collective-permute-done.23 = bf16[4,56,640]{2,1,0:T(8,128)(2,1)S(1)} collective-permute-done((bf16[4,56,640]{2,1,0:T(8,128)(2,1)S(1)}, bf16[4,56,640]{2,1,0:T(8,128)(2,1)S(1)}, u32[]{:S(2)}, u32[]{:S(2)}) %collective-permute-start.23) | collective-permute-done | bytes 286752 | tf_op jit(solution)/shard_map/ppermute | solution.py:484
  92.5 13.7 %all_to_all.5 = bf16[4,56,640]{2,1,0:T(8,128)(2,1)S(1)} all-to-all(bf16[4,56,640]{2,1,0:T(8,128)(2,1)S(1)} %broadcast_select_fusion), channel_id=1, replica_groups=mesh['segment'=2,'dp'=4,'rows'=4] {'dp'}, dimensions={0} | all-to-all | bytes 573440 | tf_op jit(solution)/shard_map/all_to_all | solution.py:685
  106.4 0.8 slice.54
  (56 shorter events, 8.3 us)
Async XLA Ops:
  0.6 1.2 %copy-start = (bf16[1,2,720,320]{2,3,1,0:T(8,128)(2,1)S(1)}, bf16[1,2,720,320]{2,3,1,0:T(8,128)(2,1)}, u32[]{:S(2)}) copy-start(bf16[1,2,720,320]{2,3,1,0:T(8,128)(2,1)} %param.11) | copy-start | bytes 2764804
  0.6 1.5 %copy-start.1 = (bf16[1,720,320]{1,2,0:T(8,128)(2,1)S(1)}, bf16[1,720,320]{1,2,0:T(8,128)(2,1)}, u32[]{:S(2)}) copy-start(bf16[1,720,320]{1,2,0:T(8,128)(2,1)} %param.12) | copy-start | bytes 1382404
  1.9 0.9 copy-start.2
  2.2 10.9 %copy-start.3 = (bf16[2,4,16,320]{3,2,1,0:T(8,128)(2,1)S(1)}, bf16[2,4,16,320]{3,2,1,0:T(8,128)(2,1)}, u32[]{:S(2)}) copy-start(bf16[2,4,16,320]{3,2,1,0:T(8,128)(2,1)} %param.8) | copy-start | bytes 245764
  2.2 10.9 %copy-start.4 = (bf16[2,4,16,320]{3,2,1,0:T(8,128)(2,1)S(1)}, bf16[2,4,16,320]{3,2,1,0:T(8,128)(2,1)}, u32[]{:S(2)}) copy-start(bf16[2,4,16,320]{3,2,1,0:T(8,128)(2,1)} %param.10) | copy-start | bytes 245764
  2.2 10.9 %copy-start.5 = (bf16[2,4,16,320]{3,2,1,0:T(8,128)(2,1)S(1)}, bf16[2,4,16,320]{3,2,1,0:T(8,128)(2,1)}, u32[]{:S(2)}) copy-start(bf16[2,4,16,320]{3,2,1,0:T(8,128)(2,1)} %param.7) | copy-start | bytes 245764
  3.0 22.5 %collective-permute-start.3 = (bf16[400,640]{1,0:T(8,128)(2,1)S(1)}, bf16[400,640]{1,0:T(8,128)(2,1)S(1)}, u32[]{:S(2)}, u32[]{:S(2)}) collective-permute-start(bf16[400,640]{1,0:T(8,128)(2,1)S(1)} %fusion.refs_4_.refs_0_), channel_id=1, source_target_pairs={{0,8},{1,9},{2,10},{4,12},{5,13},{6,14},{8,0},{9,1},{10,2},{12,4},... | collective-permute-start | bytes 1536008 | tf_op jit(solution)/shard_map/ppermute | solution.py:484
  7.5 20.8 %collective-permute-start.5 = (bf16[400,640]{1,0:T(8,128)(2,1)S(1)}, bf16[400,640]{1,0:T(8,128)(2,1)S(1)}, u32[]{:S(2)}, u32[]{:S(2)}) collective-permute-start(bf16[400,640]{1,0:T(8,128)(2,1)S(1)} %fusion.refs_4_.refs_0_), channel_id=1, source_target_pairs={{0,4},{1,5},{2,6},{4,0},{5,1},{6,2},{8,12},{9,13},{10,14},{12,8},{... | collective-permute-start | bytes 1536008 | tf_op jit(solution)/shard_map/ppermute | solution.py:484
  11.0 18.7 %collective-permute-start.4 = (bf16[400,640]{1,0:T(8,128)(2,1)S(1)}, bf16[400,640]{1,0:T(8,128)(2,1)S(1)}, u32[]{:S(2)}, u32[]{:S(2)}) collective-permute-start(bf16[400,640]{1,0:T(8,128)(2,1)S(1)} %fusion.refs_4_.refs_0_), channel_id=1, source_target_pairs={{0,12},{2,14},{4,8},{6,10},{8,4},{10,6},{12,0},{14,2},{19,31},{23,... | collective-permute-start | bytes 1536008 | tf_op jit(solution)/shard_map/ppermute | solution.py:484
  13.3 5.9 %collective-permute-start = (bf16[128,640]{1,0:T(8,128)(2,1)S(1)}, bf16[128,640]{1,0:T(8,128)(2,1)S(1)}, u32[]{:S(2)}, u32[]{:S(2)}) collective-permute-start(bf16[128,640]{1,0:T(8,128)(2,1)S(1)} %pad_maximum_fusion.1.refs_0_), channel_id=1, source_target_pairs={{0,1},{1,0},{2,3},{3,2},{4,5},{5,4},{6,7},{7,6},{8,9},{9,8},{10,11... | collective-permute-start | bytes 491528 | tf_op jit(solution)/shard_map/ppermute | solution.py:484
  13.4 7.0 %collective-permute-start.1 = (bf16[128,640]{1,0:T(8,128)(2,1)S(1)}, bf16[128,640]{1,0:T(8,128)(2,1)S(1)}, u32[]{:S(2)}, u32[]{:S(2)}) collective-permute-start(bf16[128,640]{1,0:T(8,128)(2,1)S(1)} %pad_maximum_fusion.1.refs_0_), channel_id=1, source_target_pairs={{0,2},{1,3},{2,0},{3,1},{4,6},{5,7},{6,4},{7,5},{8,10},{9,11},{10,... | collective-permute-start | bytes 491528 | tf_op jit(solution)/shard_map/ppermute | solution.py:484
  19.2 6.3 %collective-permute-start.2 = (bf16[128,640]{1,0:T(8,128)(2,1)S(1)}, bf16[128,640]{1,0:T(8,128)(2,1)}, u32[]{:S(2)}, u32[]{:S(2)}) collective-permute-start(bf16[128,640]{1,0:T(8,128)(2,1)S(1)} %pad_maximum_fusion.1.refs_0_), channel_id=1, source_target_pairs={{0,3},{1,2},{2,1},{3,0},{4,7},{5,6},{6,5},{7,4},{8,11},{9,10},{10,... | collective-permute-start | bytes 491528 | tf_op jit(solution)/shard_map/ppermute | solution.py:484
  28.3 8.4 %collective-permute-start.6 = (bf16[400,640]{1,0:T(8,128)(2,1)S(1)}, bf16[400,640]{1,0:T(8,128)(2,1)S(1)}, u32[]{:S(2)}, u32[]{:S(2)}) collective-permute-start(bf16[400,640]{1,0:T(8,128)(2,1)S(1)} %fusion.refs_4_.refs_0_), channel_id=1, source_target_pairs={{5,9},{9,5},{21,25},{25,21}} | collective-permute-start | bytes 1536008 | tf_op jit(solution)/shard_map/ppermute | solution.py:484
  29.0 8.4 %collective-permute-start.7 = (bf16[400,640]{1,0:T(8,128)(2,1)S(1)}, bf16[400,640]{1,0:T(8,128)(2,1)S(1)}, u32[]{:S(2)}, u32[]{:S(2)}) collective-permute-start(bf16[400,640]{1,0:T(8,128)(2,1)S(1)} %collective-permute-done.3.refs_5_.refs_1_), channel_id=1, source_target_pairs={{5,1},{9,13},{21,17},{25,29}} | collective-permute-start | bytes 1536008 | tf_op jit(solution)/shard_map/ppermute | solution.py:484
  33.3 5.3 %collective-permute-start.8 = (bf16[512,640]{1,0:T(8,128)(2,1)S(1)}, bf16[512,640]{1,0:T(8,128)(2,1)S(1)}, u32[]{:S(2)}, u32[]{:S(2)}) collective-permute-start(bf16[512,640]{1,0:T(8,128)(2,1)S(1)} %get-tuple-element.38), channel_id=1, source_target_pairs={{0,1},{4,5},{8,9},{12,13}} | collective-permute-start | bytes 1966088 | tf_op jit(solution)/shard_map/ppermute | solution.py:484
  34.0 6.1 %collective-permute-start.11 = (bf16[400,640]{1,0:T(8,128)(2,1)S(1)}, bf16[400,640]{1,0:T(8,128)(2,1)S(1)}, u32[]{:S(2)}, u32[]{:S(2)}) collective-permute-start(bf16[400,640]{1,0:T(8,128)(2,1)S(1)} %fusion.refs_4_.refs_0_), channel_id=1, source_target_pairs={{18,26},{22,30},{26,18},{30,22}} | collective-permute-start | bytes 1536008 | tf_op jit(solution)/shard_map/ppermute | solution.py:484
  34.7 5.3 %collective-permute-start.9 = (bf16[512,640]{1,0:T(8,128)(2,1)S(1)}, bf16[512,640]{1,0:T(8,128)(2,1)S(1)}, u32[]{:S(2)}, u32[]{:S(2)}) collective-permute-start(bf16[512,640]{1,0:T(8,128)(2,1)S(1)} %get-tuple-element.38), channel_id=1, source_target_pairs={{2,18},{6,22},{10,26},{14,30}} | collective-permute-start | bytes 1966088 | tf_op jit(solution)/shard_map/ppermute | solution.py:484
  36.6 3.5 %collective-permute-start.12 = (bf16[400,640]{1,0:T(8,128)(2,1)S(1)}, bf16[400,640]{1,0:T(8,128)(2,1)S(1)}, u32[]{:S(2)}, u32[]{:S(2)}) collective-permute-start(bf16[400,640]{1,0:T(8,128)(2,1)S(1)} %fusion.refs_4_.refs_0_), channel_id=1, source_target_pairs={{18,30},{22,26},{26,22},{30,18}} | collective-permute-start | bytes 1536008 | tf_op jit(solution)/shard_map/ppermute | solution.py:484
  37.4 2.8 %collective-permute-start.13 = (bf16[400,640]{1,0:T(8,128)(2,1)S(1)}, bf16[400,640]{1,0:T(8,128)(2,1)S(1)}, u32[]{:S(2)}, u32[]{:S(2)}) collective-permute-start(bf16[400,640]{1,0:T(8,128)(2,1)S(1)} %fusion.refs_4_.refs_0_), channel_id=1, source_target_pairs={{18,22},{22,18},{26,30},{30,26}} | collective-permute-start | bytes 1536008 | tf_op jit(solution)/shard_map/ppermute | solution.py:484
  38.6 5.4 %collective-permute-start.15 = (bf16[512,640]{1,0:T(8,128)(2,1)S(1)}, bf16[512,640]{1,0:T(8,128)(2,1)S(1)}, u32[]{:S(2)}, u32[]{:S(2)}) collective-permute-start(bf16[512,640]{1,0:T(8,128)(2,1)S(1)} %shard_map.87.sides), channel_id=1, source_target_pairs={{19,17},{23,21},{27,25},{31,29}} | collective-permute-start | bytes 1966088 | tf_op jit(solution)/shard_map/ppermute | solution.py:484
  40.7 3.4 %collective-permute-start.14 = (bf16[256,640]{1,0:T(8,128)(2,1)S(1)}, bf16[256,640]{1,0:T(8,128)(2,1)S(1)}, u32[]{:S(2)}, u32[]{:S(2)}) collective-permute-start(bf16[256,640]{1,0:T(8,128)(2,1)S(1)} %shard_map.90), channel_id=1, source_target_pairs={{18,17},{22,21},{26,25},{30,29}} | collective-permute-start | bytes 983048 | tf_op jit(solution)/shard_map/ppermute | solution.py:484
  41.4 2.7 %collective-permute-start.10 = (bf16[256,640]{1,0:T(8,128)(2,1)S(1)}, bf16[256,640]{1,0:T(8,128)(2,1)S(1)}, u32[]{:S(2)}, u32[]{:S(2)}) collective-permute-start(bf16[256,640]{1,0:T(8,128)(2,1)S(1)} %get-tuple-element.43), channel_id=1, source_target_pairs={{1,17},{5,21},{9,25},{13,29}} | collective-permute-start | bytes 983048 | tf_op jit(solution)/shard_map/ppermute | solution.py:484
  42.1 15.2 %collective-permute-start.17 = (bf16[256,640]{1,0:T(8,128)(2,1)S(1)}, bf16[256,640]{1,0:T(8,128)(2,1)S(1)}, u32[]{:S(2)}, u32[]{:S(2)}) collective-permute-start(bf16[256,640]{1,0:T(8,128)(2,1)S(1)} %get-tuple-element.48.own), channel_id=1, source_target_pairs={{0,2},{4,6},{8,10},{12,14}} | collective-permute-start | bytes 983048 | tf_op jit(solution)/shard_map/ppermute | solution.py:484
  43.4 13.9 %collective-permute-start.18 = (bf16[256,640]{1,0:T(8,128)(2,1)S(1)}, bf16[256,640]{1,0:T(8,128)(2,1)S(1)}, u32[]{:S(2)}, u32[]{:S(2)}) collective-permute-start(bf16[256,640]{1,0:T(8,128)(2,1)S(1)} %get-tuple-element.48.own), channel_id=1, source_target_pairs={{0,3},{4,7},{8,11},{12,15}} | collective-permute-start | bytes 983048 | tf_op jit(solution)/shard_map/ppermute | solution.py:484
  44.7 14.7 %collective-permute-start.16 = (bf16[256,640]{1,0:T(8,128)(2,1)S(1)}, bf16[256,640]{1,0:T(8,128)(2,1)S(1)}, u32[]{:S(2)}, u32[]{:S(2)}) collective-permute-start(bf16[256,640]{1,0:T(8,128)(2,1)S(1)} %get-tuple-element.47), channel_id=1, source_target_pairs={{17,1},{21,5},{25,9},{29,13}} | collective-permute-start | bytes 983048 | tf_op jit(solution)/shard_map/ppermute | solution.py:484
  45.3 14.0 %collective-permute-start.19 = (bf16[256,640]{1,0:T(8,128)(2,1)S(1)}, bf16[256,640]{1,0:T(8,128)(2,1)S(1)}, u32[]{:S(2)}, u32[]{:S(2)}) collective-permute-start(bf16[256,640]{1,0:T(8,128)(2,1)S(1)} %get-tuple-element.51), channel_id=1, source_target_pairs={{0,1},{4,5},{8,9},{12,13}} | collective-permute-start | bytes 983048 | tf_op jit(solution)/shard_map/ppermute | solution.py:484
  60.1 2.7 %collective-permute-start.20 = (bf16[320,640]{1,0:T(8,128)(2,1)S(1)}, bf16[320,640]{1,0:T(8,128)(2,1)S(1)}, u32[]{:S(2)}, u32[]{:S(2)}) collective-permute-start(bf16[320,640]{1,0:T(8,128)(2,1)S(1)} %get-tuple-element.58), channel_id=1, source_target_pairs={{1,0},{5,4},{9,8},{13,12}} | collective-permute-start | bytes 1228808 | tf_op jit(solution)/shard_map/ppermute | solution.py:484
  60.8 2.0 %collective-permute-start.21 = (bf16[320,640]{1,0:T(8,128)(2,1)S(1)}, bf16[320,640]{1,0:T(8,128)(2,1)S(1)}, u32[]{:S(2)}, u32[]{:S(2)}) collective-permute-start(bf16[320,640]{1,0:T(8,128)(2,1)S(1)} %get-tuple-element.57), channel_id=1, source_target_pairs={{1,3},{5,7},{9,11},{13,15}} | collective-permute-start | bytes 1228808 | tf_op jit(solution)/shard_map/ppermute | solution.py:484
  61.5 27.0 %collective-permute-start.22 = (bf16[320,640]{1,0:T(8,128)(2,1)S(1)}, bf16[320,640]{1,0:T(8,128)(2,1)S(1)}, u32[]{:S(2)}, u32[]{:S(2)}) collective-permute-start(bf16[320,640]{1,0:T(8,128)(2,1)S(1)} %get-tuple-element.56), channel_id=1, source_target_pairs={{1,2},{5,6},{9,10},{13,14}} | collective-permute-start | bytes 1228808 | tf_op jit(solution)/shard_map/ppermute | solution.py:484
  90.0 2.5 %collective-permute-start.23 = (bf16[4,56,640]{2,1,0:T(8,128)(2,1)S(1)}, bf16[4,56,640]{2,1,0:T(8,128)(2,1)S(1)}, u32[]{:S(2)}, u32[]{:S(2)}) collective-permute-start(bf16[4,56,640]{2,1,0:T(8,128)(2,1)S(1)} %get-tuple-element.55), channel_id=1, source_target_pairs={{0,16},{1,17},{2,18},{3,19},{4,20},{5,21},{6,22},{7,23},{8,24},{9,... | collective-permute-start | bytes 860168 | tf_op jit(solution)/shard_map/ppermute | solution.py:484
where the time goes:
time: 108 us
  waiting for transfers between devices  52 us (48%)
  starting transfers between devices  26.1 us (24%)
  blocking collectives  13.7 us (13%)
  Pallas kernels  10.7 us (10%)
  local copies, waits for them, and re-layouts  3.68 us (3%)
  between operations  1.18 us (1%)
    ppermute x24, waiting for transfers between devices, hop(): return lax.ppermute(values, ('segment', 'dp', 'rows'), pairs)  52 us
    ppermute x24, starting transfers between devices, hop(): return lax.ppermute(values, ('segment', 'dp', 'rows'), pairs)  26.1 us
    all_to_all x1, blocking collectives, by_roles(): total = jnp.sum(lax.all_to_all(sent, 'dp', 0, 0).astype(F32), axis=0)  13.7 us
    pallas_call x9, Pallas kernels, call(): pl.pallas_call(body, out_shape=[jax.ShapeDtypeStruct(shape, dtype) for sh...  10.7 us
  transfers between devices with their start and end apart: 24, of which 7 were waited for; matrix products, arithmetic and copies ran while one was open for 0% of the time, Pallas kernels for 8%

commit v1 on v0

--- a/solution.py
+++ b/solution.py
@@ -269,7 +269,7 @@
             view(act, n, whole, channels)[...] = silu(out).astype(BF16)
             view(bend, n, whole, channels)[...] = slope(out).astype(BF16)
 
-    @pl.when(role(ids, 0, 2))
+    @pl.when(role(ids, 0, 3))
     def _():
         place(ids, pieces, kern, maps)
         for n in range(samples):
@@ -285,7 +285,7 @@
     samples, cells, channels = images.shape[1:]
     given, extra = halves(sides)
 
-    @pl.when(role(ids, 1, 3))
+    @pl.when(role(ids, 1, 2))
     def _():
         place(ids, pieces, kern, maps)
         for n in range(samples):
@@ -338,7 +338,7 @@
     cells = wide.shape[1] - 2 * width
     near, latent = halves(near)
 
-    @pl.when(role(ids, 1, 2))
+    @pl.when(role(ids, 1, 3))
     def _():
         place(ids, pieces, kern, maps)
         for n in range(samples):
@@ -521,7 +521,7 @@
     maps = ((channels, channels), BF16)
 
     kernel = lax.dynamic_index_in_dim(
-        first_convs[0], (row % 3 == 0).astype(jnp.int32), 0, keepdims=False
+        first_convs[0], (row % 2 == 0).astype(jnp.int32), 0, keepdims=False
     )
     kernel = jnp.where(row == 1, second_convs[0], kernel)
     half = (taps + rows) // 2
@@ -531,7 +531,7 @@
         return jnp.concatenate([bundle[:half], bundle[half:]], axis=1)
 
     packed = pack(kernel, jnp.where(row == 1, pointwise_weights[0, 1], pointwise_weights[0, 0]))
-    soon, late, again = ((0, 0), (0, 2), (1, 3)), ((0, 1), (1, 1)), ((1, 2),)
+    soon, late, again = ((0, 0), (0, 3), (1, 2)), ((0, 1), (1, 1)), ((1, 3),)
     homes = soon + late
 
     def across_groups(values, k, some):
@@ -586,7 +586,7 @@
         work=us(4.4),
     )
     near = one_hop(sent, ((0, 0), (0, 1)))
-    encoded = one_hop(sent, ((0, 2), (1, 2)))
+    encoded = one_hop(sent, ((0, 3), (1, 3)))
     below = one_hop(mixed, ((0, 0), (0, 2)))
     across = one_hop(mixed, ((0, 0), (0, 3)))
     bend = one_hop(bend, ((0, 0), (0, 1)))
@@ -602,7 +602,7 @@
     kernel, back, point = call(
         layout_kernel, [kern, kern, maps], [], ids, sides, *last, work=us(2)
     )
-    sides = one_hop(sides, ((1, 3), (1, 1)))
+    sides = one_hop(sides, ((1, 2), (1, 1)))
     kernel, point, near = lax.optimization_barrier((kernel, point, near))
     out, proj = call(
         functools.partial(middle_kernel, width),
@@ -624,7 +624,7 @@
         *later,
         work=us(3.5),
     )
-    skip = one_hop(skip, ((1, 2), (1, 1)))
+    skip = one_hop(skip, ((1, 3), (1, 1)))
     moved = one_hop(proj, ((0, 1), (1, 1)))
     grad, turned = call(
         functools.partial(decoder_kernel, width, scale),

time: 108 us -> 108 us (level)
  Pallas kernels: 10.7 us -> 8.19 us
  waiting for transfers between devices: 52 us -> 53.5 us
    pallas_call x9, Pallas kernels: 10.7 us -> 8.19 us  [call(): pl.pallas_call(body, out_shape=[jax.ShapeDtypeStruct(shape, dtype) for sh...]
    ppermute x24, waiting for transfers between devices: 52 us -> 53.5 us  [hop(): return lax.ppermute(values, ('segment', 'dp', 'rows'), pairs)]
  transfers between devices with their start and end apart: 24 -> 24, of which waited for: 7 -> 6; matrix products, arithmetic and copies ran while one was open for 0% -> 0% of each run, Pallas kernels for 8% -> 6%
where the time goes in v1:
time: 108 us; the launch traced here: 107 us
  waiting for transfers between devices  53.5 us (50%)
  starting transfers between devices  26.1 us (24%)
  blocking collectives  14 us (13%)
  Pallas kernels  8.19 us (8%)
  local copies, waits for them, and re-layouts  3.69 us (3%)
  between operations  1.16 us (1%)
    ppermute x24, waiting for transfers between devices, hop(): return lax.ppermute(values, ('segment', 'dp', 'rows'), pairs)  53.5 us
    ppermute x24, starting transfers between devices, hop(): return lax.ppermute(values, ('segment', 'dp', 'rows'), pairs)  26.1 us
    all_to_all x1, blocking collectives, by_roles(): total = jnp.sum(lax.all_to_all(sent, 'dp', 0, 0).astype(F32), axis=0)  14 us
    pallas_call x9, Pallas kernels, call(): pl.pallas_call(body, out_shape=[jax.ShapeDtypeStruct(shape, dtype) for sh...  8.19 us
  transfers between devices with their start and end apart: 24, of which 6 were waited for; matrix products, arithmetic and copies ran while one was open for 0% of the time, Pallas kernels for 6%

profile of v1, /device:TPU:4, one launch (start us, length us, event | category | flops | bytes accessed | tf_op | source)
XLA Modules:
  0.0 107.3 jit_solution(8830664443851355138)
XLA Ops:
  0.7 1.2 %copy-done = bf16[1,2,720,320]{2,3,1,0:T(8,128)(2,1)S(1)} copy-done((bf16[1,2,720,320]{2,3,1,0:T(8,128)(2,1)S(1)}, bf16[1,2,720,320]{2,3,1,0:T(8,128)(2,1)}, u32[]{:S(2)}) %copy-start) | copy-done | bytes 921624
  3.0 0.7 collective-permute-start.3
  3.7 0.7 collective-permute-start.5
  4.4 0.7 collective-permute-start.4
  5.3 9.6 %collective-permute-start = (bf16[128,640]{1,0:T(8,128)(2,1)S(1)}, bf16[128,640]{1,0:T(8,128)(2,1)S(1)}, u32[]{:S(2)}, u32[]{:S(2)}) collective-permute-start(bf16[128,640]{1,0:T(8,128)(2,1)S(1)} %pad_maximum_fusion.1.refs_0_), channel_id=1, source_target_pairs={{0,1},{1,0},{2,3},{3,2},{4,5},{5,4},{6,7},{7,6},{8,9},{9,8},{10,11... | collective-permute-start | bytes 491528 | tf_op jit(solution)/shard_map/ppermute | solution.py:484
  14.9 4.6 %collective-permute-done.refs_1_ = bf16[128,640]{1,0:T(8,128)(2,1)S(1)} collective-permute-done((bf16[128,640]{1,0:T(8,128)(2,1)S(1)}, bf16[128,640]{1,0:T(8,128)(2,1)S(1)}, u32[]{:S(2)}, u32[]{:S(2)}) %collective-permute-start) | collective-permute-done | bytes 163872 | tf_op jit(solution)/shard_map/ppermute | solution.py:484
  20.2 6.0 %collective-permute-done.2.refs_3_ = bf16[128,640]{1,0:T(8,128)(2,1)} collective-permute-done((bf16[128,640]{1,0:T(8,128)(2,1)S(1)}, bf16[128,640]{1,0:T(8,128)(2,1)}, u32[]{:S(2)}, u32[]{:S(2)}) %collective-permute-start.2) | collective-permute-done | bytes 163872 | tf_op jit(solution)/shard_map/ppermute | solution.py:484
  26.2 0.7 collective-permute-start.6
  26.9 0.7 collective-permute-start.7
  27.6 1.1 %shard_map.86 = (bf16[2,2,256,320]{3,2,1,0:T(8,128)(2,1)S(1)}, bf16[512,640]{1,0:T(8,128)(2,1)S(1)}, bf16[256,640]{1,0:T(8,128)(2,1)S(1)}, bf16[256,640]{1,0:T(8,128)(2,1)S(1)}) custom-call(s32[3]{0:T(128)S(1)} %pad_add_fusion.ids, bf16[128,640]{1,0:T(8,128)(2,1)S(1)} %pad_maximum_fusion.1.refs_0_, bf16[128,640]{1,0:T(8,128)(2,1)S(1)} %collective-permute-done.refs_1_, ...), custom_call_target="tpu_custom_call" | custom-call | flops 5059999744 | tf_op jit(solution)/shard_map/pallas_call | solution.py:176
  28.8 0.7 collective-permute-start.8
  29.5 0.7 collective-permute-start.11
  30.2 0.7 collective-permute-start.9
  31.5 0.7 collective-permute-start.12
  32.2 0.7 collective-permute-start.13
  33.5 0.7 collective-permute-start.15
  34.2 0.7 shard_map.89
  35.5 0.7 collective-permute-start.14
  36.2 0.7 collective-permute-start.10
  36.9 1.3 %collective-permute-start.17 = (bf16[256,640]{1,0:T(8,128)(2,1)S(1)}, bf16[256,640]{1,0:T(8,128)(2,1)S(1)}, u32[]{:S(2)}, u32[]{:S(2)}) collective-permute-start(bf16[256,640]{1,0:T(8,128)(2,1)S(1)} %get-tuple-element.48.own), channel_id=1, source_target_pairs={{0,2},{4,6},{8,10},{12,14}} | collective-permute-start | bytes 983048 | tf_op jit(solution)/shard_map/ppermute | solution.py:484
  38.2 0.7 collective-permute-start.18
  40.9 16.4 %collective-permute-done.17.below = bf16[256,640]{1,0:T(8,128)(2,1)S(1)} collective-permute-done((bf16[256,640]{1,0:T(8,128)(2,1)S(1)}, bf16[256,640]{1,0:T(8,128)(2,1)S(1)}, u32[]{:S(2)}, u32[]{:S(2)}) %collective-permute-start.17) | collective-permute-done | bytes 327712 | tf_op jit(solution)/shard_map/ppermute | solution.py:484
  57.2 2.1 %shard_map.92.chosen = bf16[4,2,96,512]{3,2,1,0:T(8,128)(2,1)S(1)} custom-call(s32[3]{0:T(128)S(1)} %pad_add_fusion.ids, bf16[256,640]{1,0:T(8,128)(2,1)S(1)} %get-tuple-element.48.own, bf16[512,640]{1,0:T(8,128)(2,1)S(1)} %collective-permute-done.8.near, bf16[256,640]{1,0:T(8,128)(2,1)S(1)} %collective-permute-done.17.below, ...), custom_call_target="tpu_custom_call" | custom-call | flops 2300000000 | tf_op jit(solution)/shard_map/pallas_call | solution.py:176
  60.1 0.7 collective-permute-start.20
  60.8 0.7 collective-permute-start.21
  61.5 1.3 %collective-permute-start.22 = (bf16[320,640]{1,0:T(8,128)(2,1)S(1)}, bf16[320,640]{1,0:T(8,128)(2,1)S(1)}, u32[]{:S(2)}, u32[]{:S(2)}) collective-permute-start(bf16[320,640]{1,0:T(8,128)(2,1)S(1)} %get-tuple-element.56), channel_id=1, source_target_pairs={{1,2},{5,6},{9,10},{13,14}} | collective-permute-start | bytes 1228808 | tf_op jit(solution)/shard_map/ppermute | solution.py:484
  62.8 24.9 %collective-permute-done.22.third = bf16[320,640]{1,0:T(8,128)(2,1)S(1)} collective-permute-done((bf16[320,640]{1,0:T(8,128)(2,1)S(1)}, bf16[320,640]{1,0:T(8,128)(2,1)S(1)}, u32[]{:S(2)}, u32[]{:S(2)}) %collective-permute-start.22) | collective-permute-done | bytes 409632 | tf_op jit(solution)/shard_map/ppermute | solution.py:484
  87.6 1.5 %shard_map.94 = (bf16[4,56,640]{2,1,0:T(8,128)(2,1)S(1)}, bf16[4,56,640]{2,1,0:T(8,128)(2,1)S(1)}) custom-call(s32[3]{0:T(128)S(1)} %pad_add_fusion.ids, bf16[4,2,96,512]{3,2,1,0:T(8,128)(2,1)S(1)} %shard_map.92.chosen, bf16[4,320,640]{2,1,0:T(8,128)(2,1)S(1)} %shard_map.93.parcel, bf16[320,640]{1,0:T(8,128)(2,1)S(1)} %collective-permute-done.20.first, ...), custom_call_target="tpu_custom_call" | custom-call | tf_op jit(solution)/shard_map/pallas_call | solution.py:176
  89.1 1.3 %collective-permute-start.23 = (bf16[4,56,640]{2,1,0:T(8,128)(2,1)S(1)}, bf16[4,56,640]{2,1,0:T(8,128)(2,1)S(1)}, u32[]{:S(2)}, u32[]{:S(2)}) collective-permute-start(bf16[4,56,640]{2,1,0:T(8,128)(2,1)S(1)} %get-tuple-element.55), channel_id=1, source_target_pairs={{0,16},{1,17},{2,18},{3,19},{4,20},{5,21},{6,22},{7,23},{8,24},{9,... | collective-permute-start | bytes 860168 | tf_op jit(solution)/shard_map/ppermute | solution.py:484
  90.4 1.2 %collective-permute-done.23 = bf16[4,56,640]{2,1,0:T(8,128)(2,1)S(1)} collective-permute-done((bf16[4,56,640]{2,1,0:T(8,128)(2,1)S(1)}, bf16[4,56,640]{2,1,0:T(8,128)(2,1)S(1)}, u32[]{:S(2)}, u32[]{:S(2)}) %collective-permute-start.23) | collective-permute-done | bytes 286752 | tf_op jit(solution)/shard_map/ppermute | solution.py:484
  91.6 14.0 %all_to_all.5 = bf16[4,56,640]{2,1,0:T(8,128)(2,1)S(1)} all-to-all(bf16[4,56,640]{2,1,0:T(8,128)(2,1)S(1)} %broadcast_select_fusion), channel_id=1, replica_groups=mesh['segment'=2,'dp'=4,'rows'=4] {'dp'}, dimensions={0} | all-to-all | bytes 573440 | tf_op jit(solution)/shard_map/all_to_all | solution.py:685
  105.9 0.8 slice.54
  (56 shorter events, 7.2 us)
Async XLA Ops:
  0.6 1.2 %copy-start = (bf16[1,2,720,320]{2,3,1,0:T(8,128)(2,1)S(1)}, bf16[1,2,720,320]{2,3,1,0:T(8,128)(2,1)}, u32[]{:S(2)}) copy-start(bf16[1,2,720,320]{2,3,1,0:T(8,128)(2,1)} %param.11) | copy-start | bytes 2764804
  0.6 1.5 %copy-start.1 = (bf16[1,720,320]{1,2,0:T(8,128)(2,1)S(1)}, bf16[1,720,320]{1,2,0:T(8,128)(2,1)}, u32[]{:S(2)}) copy-start(bf16[1,720,320]{1,2,0:T(8,128)(2,1)} %param.12) | copy-start | bytes 1382404
  1.9 0.9 copy-start.2
  2.2 2.9 %copy-start.3 = (bf16[2,4,16,320]{3,2,1,0:T(8,128)(2,1)S(1)}, bf16[2,4,16,320]{3,2,1,0:T(8,128)(2,1)}, u32[]{:S(2)}) copy-start(bf16[2,4,16,320]{3,2,1,0:T(8,128)(2,1)} %param.8) | copy-start | bytes 245764
  2.2 2.9 %copy-start.4 = (bf16[2,4,16,320]{3,2,1,0:T(8,128)(2,1)S(1)}, bf16[2,4,16,320]{3,2,1,0:T(8,128)(2,1)}, u32[]{:S(2)}) copy-start(bf16[2,4,16,320]{3,2,1,0:T(8,128)(2,1)} %param.10) | copy-start | bytes 245764
  2.2 2.9 %copy-start.5 = (bf16[2,4,16,320]{3,2,1,0:T(8,128)(2,1)S(1)}, bf16[2,4,16,320]{3,2,1,0:T(8,128)(2,1)}, u32[]{:S(2)}) copy-start(bf16[2,4,16,320]{3,2,1,0:T(8,128)(2,1)} %param.7) | copy-start | bytes 245764
  3.0 23.2 %collective-permute-start.3 = (bf16[400,640]{1,0:T(8,128)(2,1)S(1)}, bf16[400,640]{1,0:T(8,128)(2,1)S(1)}, u32[]{:S(2)}, u32[]{:S(2)}) collective-permute-start(bf16[400,640]{1,0:T(8,128)(2,1)S(1)} %fusion.refs_4_.refs_0_), channel_id=1, source_target_pairs={{0,8},{1,9},{3,11},{4,12},{5,13},{7,15},{8,0},{9,1},{11,3},{12,4},... | collective-permute-start | bytes 1536008 | tf_op jit(solution)/shard_map/ppermute | solution.py:484
  3.7 22.5 %collective-permute-start.5 = (bf16[400,640]{1,0:T(8,128)(2,1)S(1)}, bf16[400,640]{1,0:T(8,128)(2,1)S(1)}, u32[]{:S(2)}, u32[]{:S(2)}) collective-permute-start(bf16[400,640]{1,0:T(8,128)(2,1)S(1)} %fusion.refs_4_.refs_0_), channel_id=1, source_target_pairs={{0,4},{1,5},{3,7},{4,0},{5,1},{7,3},{8,12},{9,13},{11,15},{12,8},{... | collective-permute-start | bytes 1536008 | tf_op jit(solution)/shard_map/ppermute | solution.py:484
  4.4 23.2 %collective-permute-start.4 = (bf16[400,640]{1,0:T(8,128)(2,1)S(1)}, bf16[400,640]{1,0:T(8,128)(2,1)S(1)}, u32[]{:S(2)}, u32[]{:S(2)}) collective-permute-start(bf16[400,640]{1,0:T(8,128)(2,1)S(1)} %fusion.refs_4_.refs_0_), channel_id=1, source_target_pairs={{0,12},{3,15},{4,8},{7,11},{8,4},{11,7},{12,0},{15,3},{18,30},{22,... | collective-permute-start | bytes 1536008 | tf_op jit(solution)/shard_map/ppermute | solution.py:484
  5.3 14.2 %collective-permute-start = (bf16[128,640]{1,0:T(8,128)(2,1)S(1)}, bf16[128,640]{1,0:T(8,128)(2,1)S(1)}, u32[]{:S(2)}, u32[]{:S(2)}) collective-permute-start(bf16[128,640]{1,0:T(8,128)(2,1)S(1)} %pad_maximum_fusion.1.refs_0_), channel_id=1, source_target_pairs={{0,1},{1,0},{2,3},{3,2},{4,5},{5,4},{6,7},{7,6},{8,9},{9,8},{10,11... | collective-permute-start | bytes 491528 | tf_op jit(solution)/shard_map/ppermute | solution.py:484
  14.9 5.3 %collective-permute-start.1 = (bf16[128,640]{1,0:T(8,128)(2,1)S(1)}, bf16[128,640]{1,0:T(8,128)(2,1)S(1)}, u32[]{:S(2)}, u32[]{:S(2)}) collective-permute-start(bf16[128,640]{1,0:T(8,128)(2,1)S(1)} %pad_maximum_fusion.1.refs_0_), channel_id=1, source_target_pairs={{0,2},{1,3},{2,0},{3,1},{4,6},{5,7},{6,4},{7,5},{8,10},{9,11},{10,... | collective-permute-start | bytes 491528 | tf_op jit(solution)/shard_map/ppermute | solution.py:484
  19.4 6.8 %collective-permute-start.2 = (bf16[128,640]{1,0:T(8,128)(2,1)S(1)}, bf16[128,640]{1,0:T(8,128)(2,1)}, u32[]{:S(2)}, u32[]{:S(2)}) collective-permute-start(bf16[128,640]{1,0:T(8,128)(2,1)S(1)} %pad_maximum_fusion.1.refs_0_), channel_id=1, source_target_pairs={{0,3},{1,2},{2,1},{3,0},{4,7},{5,6},{6,5},{7,4},{8,11},{9,10},{10,... | collective-permute-start | bytes 491528 | tf_op jit(solution)/shard_map/ppermute | solution.py:484
  26.2 5.2 %collective-permute-start.6 = (bf16[400,640]{1,0:T(8,128)(2,1)S(1)}, bf16[400,640]{1,0:T(8,128)(2,1)S(1)}, u32[]{:S(2)}, u32[]{:S(2)}) collective-permute-start(bf16[400,640]{1,0:T(8,128)(2,1)S(1)} %fusion.refs_4_.refs_0_), channel_id=1, source_target_pairs={{5,9},{9,5},{21,25},{25,21}} | collective-permute-start | bytes 1536008 | tf_op jit(solution)/shard_map/ppermute | solution.py:484
  26.9 5.3 %collective-permute-start.7 = (bf16[400,640]{1,0:T(8,128)(2,1)S(1)}, bf16[400,640]{1,0:T(8,128)(2,1)S(1)}, u32[]{:S(2)}, u32[]{:S(2)}) collective-permute-start(bf16[400,640]{1,0:T(8,128)(2,1)S(1)} %collective-permute-done.3.refs_5_.refs_1_), channel_id=1, source_target_pairs={{5,1},{9,13},{21,17},{25,29}} | collective-permute-start | bytes 1536008 | tf_op jit(solution)/shard_map/ppermute | solution.py:484
  28.8 4.7 %collective-permute-start.8 = (bf16[512,640]{1,0:T(8,128)(2,1)S(1)}, bf16[512,640]{1,0:T(8,128)(2,1)S(1)}, u32[]{:S(2)}, u32[]{:S(2)}) collective-permute-start(bf16[512,640]{1,0:T(8,128)(2,1)S(1)} %get-tuple-element.38), channel_id=1, source_target_pairs={{0,1},{4,5},{8,9},{12,13}} | collective-permute-start | bytes 1966088 | tf_op jit(solution)/shard_map/ppermute | solution.py:484
  29.5 5.4 %collective-permute-start.11 = (bf16[400,640]{1,0:T(8,128)(2,1)S(1)}, bf16[400,640]{1,0:T(8,128)(2,1)S(1)}, u32[]{:S(2)}, u32[]{:S(2)}) collective-permute-start(bf16[400,640]{1,0:T(8,128)(2,1)S(1)} %fusion.refs_4_.refs_0_), channel_id=1, source_target_pairs={{19,27},{23,31},{27,19},{31,23}} | collective-permute-start | bytes 1536008 | tf_op jit(solution)/shard_map/ppermute | solution.py:484
  30.2 4.7 %collective-permute-start.9 = (bf16[512,640]{1,0:T(8,128)(2,1)S(1)}, bf16[512,640]{1,0:T(8,128)(2,1)S(1)}, u32[]{:S(2)}, u32[]{:S(2)}) collective-permute-start(bf16[512,640]{1,0:T(8,128)(2,1)S(1)} %get-tuple-element.38), channel_id=1, source_target_pairs={{3,19},{7,23},{11,27},{15,31}} | collective-permute-start | bytes 1966088 | tf_op jit(solution)/shard_map/ppermute | solution.py:484
  31.5 3.5 %collective-permute-start.12 = (bf16[400,640]{1,0:T(8,128)(2,1)S(1)}, bf16[400,640]{1,0:T(8,128)(2,1)S(1)}, u32[]{:S(2)}, u32[]{:S(2)}) collective-permute-start(bf16[400,640]{1,0:T(8,128)(2,1)S(1)} %fusion.refs_4_.refs_0_), channel_id=1, source_target_pairs={{19,31},{23,27},{27,23},{31,19}} | collective-permute-start | bytes 1536008 | tf_op jit(solution)/shard_map/ppermute | solution.py:484
  32.2 2.8 %collective-permute-start.13 = (bf16[400,640]{1,0:T(8,128)(2,1)S(1)}, bf16[400,640]{1,0:T(8,128)(2,1)S(1)}, u32[]{:S(2)}, u32[]{:S(2)}) collective-permute-start(bf16[400,640]{1,0:T(8,128)(2,1)S(1)} %fusion.refs_4_.refs_0_), channel_id=1, source_target_pairs={{19,23},{23,19},{27,31},{31,27}} | collective-permute-start | bytes 1536008 | tf_op jit(solution)/shard_map/ppermute | solution.py:484
  33.5 5.4 %collective-permute-start.15 = (bf16[512,640]{1,0:T(8,128)(2,1)S(1)}, bf16[512,640]{1,0:T(8,128)(2,1)S(1)}, u32[]{:S(2)}, u32[]{:S(2)}) collective-permute-start(bf16[512,640]{1,0:T(8,128)(2,1)S(1)} %shard_map.87.sides), channel_id=1, source_target_pairs={{18,17},{22,21},{26,25},{30,29}} | collective-permute-start | bytes 1966088 | tf_op jit(solution)/shard_map/ppermute | solution.py:484
  35.5 3.4 %collective-permute-start.14 = (bf16[256,640]{1,0:T(8,128)(2,1)S(1)}, bf16[256,640]{1,0:T(8,128)(2,1)S(1)}, u32[]{:S(2)}, u32[]{:S(2)}) collective-permute-start(bf16[256,640]{1,0:T(8,128)(2,1)S(1)} %shard_map.90), channel_id=1, source_target_pairs={{19,17},{23,21},{27,25},{31,29}} | collective-permute-start | bytes 983048 | tf_op jit(solution)/shard_map/ppermute | solution.py:484
  36.2 2.7 %collective-permute-start.10 = (bf16[256,640]{1,0:T(8,128)(2,1)S(1)}, bf16[256,640]{1,0:T(8,128)(2,1)S(1)}, u32[]{:S(2)}, u32[]{:S(2)}) collective-permute-start(bf16[256,640]{1,0:T(8,128)(2,1)S(1)} %get-tuple-element.43), channel_id=1, source_target_pairs={{1,17},{5,21},{9,25},{13,29}} | collective-permute-start | bytes 983048 | tf_op jit(solution)/shard_map/ppermute | solution.py:484
  36.9 20.4 %collective-permute-start.17 = (bf16[256,640]{1,0:T(8,128)(2,1)S(1)}, bf16[256,640]{1,0:T(8,128)(2,1)S(1)}, u32[]{:S(2)}, u32[]{:S(2)}) collective-permute-start(bf16[256,640]{1,0:T(8,128)(2,1)S(1)} %get-tuple-element.48.own), channel_id=1, source_target_pairs={{0,2},{4,6},{8,10},{12,14}} | collective-permute-start | bytes 983048 | tf_op jit(solution)/shard_map/ppermute | solution.py:484
  38.2 19.1 %collective-permute-start.18 = (bf16[256,640]{1,0:T(8,128)(2,1)S(1)}, bf16[256,640]{1,0:T(8,128)(2,1)S(1)}, u32[]{:S(2)}, u32[]{:S(2)}) collective-permute-start(bf16[256,640]{1,0:T(8,128)(2,1)S(1)} %get-tuple-element.48.own), channel_id=1, source_target_pairs={{0,3},{4,7},{8,11},{12,15}} | collective-permute-start | bytes 983048 | tf_op jit(solution)/shard_map/ppermute | solution.py:484
  39.5 19.9 %collective-permute-start.16 = (bf16[256,640]{1,0:T(8,128)(2,1)S(1)}, bf16[256,640]{1,0:T(8,128)(2,1)S(1)}, u32[]{:S(2)}, u32[]{:S(2)}) collective-permute-start(bf16[256,640]{1,0:T(8,128)(2,1)S(1)} %get-tuple-element.47), channel_id=1, source_target_pairs={{17,1},{21,5},{25,9},{29,13}} | collective-permute-start | bytes 983048 | tf_op jit(solution)/shard_map/ppermute | solution.py:484
  40.2 19.2 %collective-permute-start.19 = (bf16[256,640]{1,0:T(8,128)(2,1)S(1)}, bf16[256,640]{1,0:T(8,128)(2,1)S(1)}, u32[]{:S(2)}, u32[]{:S(2)}) collective-permute-start(bf16[256,640]{1,0:T(8,128)(2,1)S(1)} %get-tuple-element.51), channel_id=1, source_target_pairs={{0,1},{4,5},{8,9},{12,13}} | collective-permute-start | bytes 983048 | tf_op jit(solution)/shard_map/ppermute | solution.py:484
  60.1 2.7 %collective-permute-start.20 = (bf16[320,640]{1,0:T(8,128)(2,1)S(1)}, bf16[320,640]{1,0:T(8,128)(2,1)S(1)}, u32[]{:S(2)}, u32[]{:S(2)}) collective-permute-start(bf16[320,640]{1,0:T(8,128)(2,1)S(1)} %get-tuple-element.58), channel_id=1, source_target_pairs={{1,0},{5,4},{9,8},{13,12}} | collective-permute-start | bytes 1228808 | tf_op jit(solution)/shard_map/ppermute | solution.py:484
  60.8 2.0 %collective-permute-start.21 = (bf16[320,640]{1,0:T(8,128)(2,1)S(1)}, bf16[320,640]{1,0:T(8,128)(2,1)S(1)}, u32[]{:S(2)}, u32[]{:S(2)}) collective-permute-start(bf16[320,640]{1,0:T(8,128)(2,1)S(1)} %get-tuple-element.57), channel_id=1, source_target_pairs={{1,3},{5,7},{9,11},{13,15}} | collective-permute-start | bytes 1228808 | tf_op jit(solution)/shard_map/ppermute | solution.py:484
  61.5 26.2 %collective-permute-start.22 = (bf16[320,640]{1,0:T(8,128)(2,1)S(1)}, bf16[320,640]{1,0:T(8,128)(2,1)S(1)}, u32[]{:S(2)}, u32[]{:S(2)}) collective-permute-start(bf16[320,640]{1,0:T(8,128)(2,1)S(1)} %get-tuple-element.56), channel_id=1, source_target_pairs={{1,2},{5,6},{9,10},{13,14}} | collective-permute-start | bytes 1228808 | tf_op jit(solution)/shard_map/ppermute | solution.py:484
  89.1 2.5 %collective-permute-start.23 = (bf16[4,56,640]{2,1,0:T(8,128)(2,1)S(1)}, bf16[4,56,640]{2,1,0:T(8,128)(2,1)S(1)}, u32[]{:S(2)}, u32[]{:S(2)}) collective-permute-start(bf16[4,56,640]{2,1,0:T(8,128)(2,1)S(1)} %get-tuple-element.55), channel_id=1, source_target_pairs={{0,16},{1,17},{2,18},{3,19},{4,20},{5,21},{6,22},{7,23},{8,24},{9,... | collective-permute-start | bytes 860168 | tf_op jit(solution)/shard_map/ppermute | solution.py:484

commit v2 on v1

--- a/solution.py
+++ b/solution.py
@@ -332,8 +332,8 @@
 
 
 def skip_kernel(width, ids, near, *refs):
-    pieces = refs[:4]
-    skip, kern, maps, wide = refs[4:]
+    pieces = refs[:5]
+    skip, kern, maps, wide = refs[5:]
     samples, channels = wide.shape[0], wide.shape[2] // 3
     cells = wide.shape[1] - 2 * width
     near, latent = halves(near)
@@ -549,16 +549,22 @@
 
     early = (packed, two, across_groups(packed, 3, soon), one)
     tied, *others = lax.optimization_barrier((packed, *others))
-    later = (tied, *(across_groups(tied, k, again) for k in (2, 3, 1)))
+
+    def second_phase(own, far, some):
+        return [
+            hop(
+                values,
+                sizes,
+                lambda s, d, r: (s, d ^ k, r) if (s, r) in some and d in (1, 2) else None,
+            )
+            for k, values in ((3, own), (1, far))
+        ]
+
+    far, beside = (across_groups(tied, k, again) for k in (2, 1))
+    ends = second_phase(tied, far, again)
+    later = (tied, far, ends[0], beside, ends[1])
     two, one, direct = lax.optimization_barrier((two, one, packed))
-    ends = [
-        hop(
-            values,
-            sizes,
-            lambda s, d, r: (s, d ^ k, r) if (s, r) in late and d in (1, 2) else None,
-        )
-        for k, values in ((3, direct), (1, two))
-    ]
+    ends = second_phase(direct, two, late)
     last = (direct, two, ends[0], one, ends[1])
 
     def one_hop(values, *moves):

time: 108 us -> 113 us (1.046)
  waiting for transfers between devices: 53.5 us -> 58.5 us
    ppermute x24 -> x25, waiting for transfers between devices: 53.5 us -> 58.5 us  [hop(): return lax.ppermute(values, ('segment', 'dp', 'rows'), pairs)]
    ppermute x24 -> x25, starting transfers between devices: 26.1 us -> 26.8 us  [hop(): return lax.ppermute(values, ('segment', 'dp', 'rows'), pairs)]
  transfers between devices with their start and end apart: 24 -> 25, of which waited for: 6 -> 6; matrix products, arithmetic and copies ran while one was open for 0% -> 0% of each run, Pallas kernels for 6% -> 5%
where the time goes in v2:
time: 113 us
  waiting for transfers between devices  58.5 us (52%)
  starting transfers between devices  26.8 us (24%)
  blocking collectives  13.9 us (12%)
  Pallas kernels  8.19 us (7%)
  local copies, waits for them, and re-layouts  3.69 us (3%)
  between operations  1.19 us (1%)
    ppermute x25, waiting for transfers between devices, hop(): return lax.ppermute(values, ('segment', 'dp', 'rows'), pairs)  58.5 us
    ppermute x25, starting transfers between devices, hop(): return lax.ppermute(values, ('segment', 'dp', 'rows'), pairs)  26.8 us
    all_to_all x1, blocking collectives, by_roles(): total = jnp.sum(lax.all_to_all(sent, 'dp', 0, 0).astype(F32), axis=0)  13.9 us
    pallas_call x9, Pallas kernels, call(): pl.pallas_call(body, out_shape=[jax.ShapeDtypeStruct(shape, dtype) for sh...  8.19 us
  transfers between devices with their start and end apart: 25, of which 6 were waited for; matrix products, arithmetic and copies ran while one was open for 0% of the time, Pallas kernels for 5%

profile of v2, /device:TPU:4, one launch (start us, length us, event | category | flops | bytes accessed | tf_op | source)
XLA Modules:
  0.0 112.9 jit_solution(336507855450423846)
XLA Ops:
  0.7 1.2 %copy-done = bf16[1,2,720,320]{2,3,1,0:T(8,128)(2,1)S(1)} copy-done((bf16[1,2,720,320]{2,3,1,0:T(8,128)(2,1)S(1)}, bf16[1,2,720,320]{2,3,1,0:T(8,128)(2,1)}, u32[]{:S(2)}) %copy-start) | copy-done | bytes 921624
  3.0 0.7 collective-permute-start.3
  3.7 0.7 collective-permute-start.5
  4.4 0.7 collective-permute-start.4
  5.3 9.6 %collective-permute-start = (bf16[128,640]{1,0:T(8,128)(2,1)S(1)}, bf16[128,640]{1,0:T(8,128)(2,1)S(1)}, u32[]{:S(2)}, u32[]{:S(2)}) collective-permute-start(bf16[128,640]{1,0:T(8,128)(2,1)S(1)} %pad_maximum_fusion.1.refs_0_), channel_id=1, source_target_pairs={{0,1},{1,0},{2,3},{3,2},{4,5},{5,4},{6,7},{7,6},{8,9},{9,8},{10,11... | collective-permute-start | bytes 491528 | tf_op jit(solution)/shard_map/ppermute | solution.py:484
  14.9 4.6 %collective-permute-done.refs_1_ = bf16[128,640]{1,0:T(8,128)(2,1)S(1)} collective-permute-done((bf16[128,640]{1,0:T(8,128)(2,1)S(1)}, bf16[128,640]{1,0:T(8,128)(2,1)S(1)}, u32[]{:S(2)}, u32[]{:S(2)}) %collective-permute-start) | collective-permute-done | bytes 163872 | tf_op jit(solution)/shard_map/ppermute | solution.py:484
  20.2 6.0 %collective-permute-done.2.refs_3_ = bf16[128,640]{1,0:T(8,128)(2,1)} collective-permute-done((bf16[128,640]{1,0:T(8,128)(2,1)S(1)}, bf16[128,640]{1,0:T(8,128)(2,1)}, u32[]{:S(2)}, u32[]{:S(2)}) %collective-permute-start.2) | collective-permute-done | bytes 163872 | tf_op jit(solution)/shard_map/ppermute | solution.py:484
  26.2 0.7 collective-permute-start.11
  26.9 0.7 collective-permute-start.6
  27.6 0.7 collective-permute-start.7
  28.4 1.1 %shard_map.86 = (bf16[2,2,256,320]{3,2,1,0:T(8,128)(2,1)S(1)}, bf16[512,640]{1,0:T(8,128)(2,1)S(1)}, bf16[256,640]{1,0:T(8,128)(2,1)S(1)}, bf16[256,640]{1,0:T(8,128)(2,1)S(1)}) custom-call(s32[3]{0:T(128)S(1)} %pad_add_fusion.ids, bf16[128,640]{1,0:T(8,128)(2,1)S(1)} %pad_maximum_fusion.1.refs_0_, bf16[128,640]{1,0:T(8,128)(2,1)S(1)} %collective-permute-done.refs_1_, ...), custom_call_target="tpu_custom_call" | custom-call | flops 5059999744 | tf_op jit(solution)/shard_map/pallas_call | solution.py:176
  29.5 0.7 collective-permute-start.8
  30.2 0.7 collective-permute-start.9
  31.5 0.7 collective-permute-start.12
  32.2 0.7 collective-permute-start.13
  32.9 0.7 collective-permute-start.14
  34.2 0.7 collective-permute-start.16
  34.9 0.7 shard_map.89
  35.6 0.7 collective-permute-start.10
  36.9 0.7 collective-permute-start.15
  37.6 1.3 %collective-permute-start.18 = (bf16[256,640]{1,0:T(8,128)(2,1)S(1)}, bf16[256,640]{1,0:T(8,128)(2,1)S(1)}, u32[]{:S(2)}, u32[]{:S(2)}) collective-permute-start(bf16[256,640]{1,0:T(8,128)(2,1)S(1)} %get-tuple-element.48.own), channel_id=1, source_target_pairs={{0,2},{4,6},{8,10},{12,14}} | collective-permute-start | bytes 983048 | tf_op jit(solution)/shard_map/ppermute | solution.py:484
  41.6 15.7 %collective-permute-done.18.below = bf16[256,640]{1,0:T(8,128)(2,1)S(1)} collective-permute-done((bf16[256,640]{1,0:T(8,128)(2,1)S(1)}, bf16[256,640]{1,0:T(8,128)(2,1)S(1)}, u32[]{:S(2)}, u32[]{:S(2)}) %collective-permute-start.18) | collective-permute-done | bytes 327712 | tf_op jit(solution)/shard_map/ppermute | solution.py:484
  57.2 2.1 %shard_map.92.chosen = bf16[4,2,96,512]{3,2,1,0:T(8,128)(2,1)S(1)} custom-call(s32[3]{0:T(128)S(1)} %pad_add_fusion.ids, bf16[256,640]{1,0:T(8,128)(2,1)S(1)} %get-tuple-element.48.own, bf16[512,640]{1,0:T(8,128)(2,1)S(1)} %collective-permute-done.8.near, bf16[256,640]{1,0:T(8,128)(2,1)S(1)} %collective-permute-done.18.below, ...), custom_call_target="tpu_custom_call" | custom-call | flops 2300000000 | tf_op jit(solution)/shard_map/pallas_call | solution.py:176
  60.1 0.7 collective-permute-start.21
  60.8 0.7 collective-permute-start.22
  61.5 1.3 %collective-permute-start.23 = (bf16[320,640]{1,0:T(8,128)(2,1)S(1)}, bf16[320,640]{1,0:T(8,128)(2,1)S(1)}, u32[]{:S(2)}, u32[]{:S(2)}) collective-permute-start(bf16[320,640]{1,0:T(8,128)(2,1)S(1)} %get-tuple-element.56), channel_id=1, source_target_pairs={{1,2},{5,6},{9,10},{13,14}} | collective-permute-start | bytes 1228808 | tf_op jit(solution)/shard_map/ppermute | solution.py:484
  62.8 30.6 %collective-permute-done.23.third = bf16[320,640]{1,0:T(8,128)(2,1)S(1)} collective-permute-done((bf16[320,640]{1,0:T(8,128)(2,1)S(1)}, bf16[320,640]{1,0:T(8,128)(2,1)S(1)}, u32[]{:S(2)}, u32[]{:S(2)}) %collective-permute-start.23) | collective-permute-done | bytes 409632 | tf_op jit(solution)/shard_map/ppermute | solution.py:484
  93.3 1.5 %shard_map.94 = (bf16[4,56,640]{2,1,0:T(8,128)(2,1)S(1)}, bf16[4,56,640]{2,1,0:T(8,128)(2,1)S(1)}) custom-call(s32[3]{0:T(128)S(1)} %pad_add_fusion.ids, bf16[4,2,96,512]{3,2,1,0:T(8,128)(2,1)S(1)} %shard_map.92.chosen, bf16[4,320,640]{2,1,0:T(8,128)(2,1)S(1)} %shard_map.93.parcel, bf16[320,640]{1,0:T(8,128)(2,1)S(1)} %collective-permute-done.21.first, ...), custom_call_target="tpu_custom_call" | custom-call | tf_op jit(solution)/shard_map/pallas_call | solution.py:176
  94.8 1.3 %collective-permute-start.24 = (bf16[4,56,640]{2,1,0:T(8,128)(2,1)S(1)}, bf16[4,56,640]{2,1,0:T(8,128)(2,1)S(1)}, u32[]{:S(2)}, u32[]{:S(2)}) collective-permute-start(bf16[4,56,640]{2,1,0:T(8,128)(2,1)S(1)} %get-tuple-element.55), channel_id=1, source_target_pairs={{0,16},{1,17},{2,18},{3,19},{4,20},{5,21},{6,22},{7,23},{8,24},{9,... | collective-permute-start | bytes 860168 | tf_op jit(solution)/shard_map/ppermute | solution.py:484
  96.1 1.2 %collective-permute-done.24 = bf16[4,56,640]{2,1,0:T(8,128)(2,1)S(1)} collective-permute-done((bf16[4,56,640]{2,1,0:T(8,128)(2,1)S(1)}, bf16[4,56,640]{2,1,0:T(8,128)(2,1)S(1)}, u32[]{:S(2)}, u32[]{:S(2)}) %collective-permute-start.24) | collective-permute-done | bytes 286752 | tf_op jit(solution)/shard_map/ppermute | solution.py:484
  97.3 13.9 %all_to_all.5 = bf16[4,56,640]{2,1,0:T(8,128)(2,1)S(1)} all-to-all(bf16[4,56,640]{2,1,0:T(8,128)(2,1)S(1)} %broadcast_select_fusion), channel_id=1, replica_groups=mesh['segment'=2,'dp'=4,'rows'=4] {'dp'}, dimensions={0} | all-to-all | bytes 573440 | tf_op jit(solution)/shard_map/all_to_all | solution.py:691
  111.5 0.8 slice.54
  (58 shorter events, 7.9 us)
Async XLA Ops:
  0.6 1.2 %copy-start = (bf16[1,2,720,320]{2,3,1,0:T(8,128)(2,1)S(1)}, bf16[1,2,720,320]{2,3,1,0:T(8,128)(2,1)}, u32[]{:S(2)}) copy-start(bf16[1,2,720,320]{2,3,1,0:T(8,128)(2,1)} %param.11) | copy-start | bytes 2764804
  0.6 1.5 %copy-start.1 = (bf16[1,720,320]{1,2,0:T(8,128)(2,1)S(1)}, bf16[1,720,320]{1,2,0:T(8,128)(2,1)}, u32[]{:S(2)}) copy-start(bf16[1,720,320]{1,2,0:T(8,128)(2,1)} %param.12) | copy-start | bytes 1382404
  1.9 0.9 copy-start.2
  2.2 2.9 %copy-start.3 = (bf16[2,4,16,320]{3,2,1,0:T(8,128)(2,1)S(1)}, bf16[2,4,16,320]{3,2,1,0:T(8,128)(2,1)}, u32[]{:S(2)}) copy-start(bf16[2,4,16,320]{3,2,1,0:T(8,128)(2,1)} %param.8) | copy-start | bytes 245764
  2.2 2.9 %copy-start.4 = (bf16[2,4,16,320]{3,2,1,0:T(8,128)(2,1)S(1)}, bf16[2,4,16,320]{3,2,1,0:T(8,128)(2,1)}, u32[]{:S(2)}) copy-start(bf16[2,4,16,320]{3,2,1,0:T(8,128)(2,1)} %param.10) | copy-start | bytes 245764
  2.2 2.9 %copy-start.5 = (bf16[2,4,16,320]{3,2,1,0:T(8,128)(2,1)S(1)}, bf16[2,4,16,320]{3,2,1,0:T(8,128)(2,1)}, u32[]{:S(2)}) copy-start(bf16[2,4,16,320]{3,2,1,0:T(8,128)(2,1)} %param.7) | copy-start | bytes 245764
  3.0 23.9 %collective-permute-start.3 = (bf16[400,640]{1,0:T(8,128)(2,1)S(1)}, bf16[400,640]{1,0:T(8,128)(2,1)S(1)}, u32[]{:S(2)}, u32[]{:S(2)}) collective-permute-start(bf16[400,640]{1,0:T(8,128)(2,1)S(1)} %fusion.refs_4_.refs_0_), channel_id=1, source_target_pairs={{0,8},{1,9},{3,11},{4,12},{5,13},{7,15},{8,0},{9,1},{11,3},{12,4},... | collective-permute-start | bytes 1536008 | tf_op jit(solution)/shard_map/ppermute | solution.py:484
  3.7 23.2 %collective-permute-start.5 = (bf16[400,640]{1,0:T(8,128)(2,1)S(1)}, bf16[400,640]{1,0:T(8,128)(2,1)S(1)}, u32[]{:S(2)}, u32[]{:S(2)}) collective-permute-start(bf16[400,640]{1,0:T(8,128)(2,1)S(1)} %fusion.refs_4_.refs_0_), channel_id=1, source_target_pairs={{0,4},{1,5},{3,7},{4,0},{5,1},{7,3},{8,12},{9,13},{11,15},{12,8},{... | collective-permute-start | bytes 1536008 | tf_op jit(solution)/shard_map/ppermute | solution.py:484
  4.4 24.0 %collective-permute-start.4 = (bf16[400,640]{1,0:T(8,128)(2,1)S(1)}, bf16[400,640]{1,0:T(8,128)(2,1)S(1)}, u32[]{:S(2)}, u32[]{:S(2)}) collective-permute-start(bf16[400,640]{1,0:T(8,128)(2,1)S(1)} %fusion.refs_4_.refs_0_), channel_id=1, source_target_pairs={{0,12},{3,15},{4,8},{7,11},{8,4},{11,7},{12,0},{15,3},{18,30},{22,... | collective-permute-start | bytes 1536008 | tf_op jit(solution)/shard_map/ppermute | solution.py:484
  5.3 14.2 %collective-permute-start = (bf16[128,640]{1,0:T(8,128)(2,1)S(1)}, bf16[128,640]{1,0:T(8,128)(2,1)S(1)}, u32[]{:S(2)}, u32[]{:S(2)}) collective-permute-start(bf16[128,640]{1,0:T(8,128)(2,1)S(1)} %pad_maximum_fusion.1.refs_0_), channel_id=1, source_target_pairs={{0,1},{1,0},{2,3},{3,2},{4,5},{5,4},{6,7},{7,6},{8,9},{9,8},{10,11... | collective-permute-start | bytes 491528 | tf_op jit(solution)/shard_map/ppermute | solution.py:484
  14.9 5.3 %collective-permute-start.1 = (bf16[128,640]{1,0:T(8,128)(2,1)S(1)}, bf16[128,640]{1,0:T(8,128)(2,1)S(1)}, u32[]{:S(2)}, u32[]{:S(2)}) collective-permute-start(bf16[128,640]{1,0:T(8,128)(2,1)S(1)} %pad_maximum_fusion.1.refs_0_), channel_id=1, source_target_pairs={{0,2},{1,3},{2,0},{3,1},{4,6},{5,7},{6,4},{7,5},{8,10},{9,11},{10,... | collective-permute-start | bytes 491528 | tf_op jit(solution)/shard_map/ppermute | solution.py:484
  19.4 6.8 %collective-permute-start.2 = (bf16[128,640]{1,0:T(8,128)(2,1)S(1)}, bf16[128,640]{1,0:T(8,128)(2,1)}, u32[]{:S(2)}, u32[]{:S(2)}) collective-permute-start(bf16[128,640]{1,0:T(8,128)(2,1)S(1)} %pad_maximum_fusion.1.refs_0_), channel_id=1, source_target_pairs={{0,3},{1,2},{2,1},{3,0},{4,7},{5,6},{6,5},{7,4},{8,11},{9,10},{10,... | collective-permute-start | bytes 491528 | tf_op jit(solution)/shard_map/ppermute | solution.py:484
  26.2 5.3 %collective-permute-start.11 = (bf16[400,640]{1,0:T(8,128)(2,1)S(1)}, bf16[400,640]{1,0:T(8,128)(2,1)S(1)}, u32[]{:S(2)}, u32[]{:S(2)}) collective-permute-start(bf16[400,640]{1,0:T(8,128)(2,1)S(1)} %fusion.refs_4_.refs_0_), channel_id=1, source_target_pairs={{19,27},{23,31},{27,19},{31,23}} | collective-permute-start | bytes 1536008 | tf_op jit(solution)/shard_map/ppermute | solution.py:484
  26.9 5.3 %collective-permute-start.6 = (bf16[400,640]{1,0:T(8,128)(2,1)S(1)}, bf16[400,640]{1,0:T(8,128)(2,1)S(1)}, u32[]{:S(2)}, u32[]{:S(2)}) collective-permute-start(bf16[400,640]{1,0:T(8,128)(2,1)S(1)} %fusion.refs_4_.refs_0_), channel_id=1, source_target_pairs={{5,9},{9,5},{21,25},{25,21}} | collective-permute-start | bytes 1536008 | tf_op jit(solution)/shard_map/ppermute | solution.py:484
  27.6 5.3 %collective-permute-start.7 = (bf16[400,640]{1,0:T(8,128)(2,1)S(1)}, bf16[400,640]{1,0:T(8,128)(2,1)S(1)}, u32[]{:S(2)}, u32[]{:S(2)}) collective-permute-start(bf16[400,640]{1,0:T(8,128)(2,1)S(1)} %collective-permute-done.3.refs_5_.refs_1_), channel_id=1, source_target_pairs={{5,1},{9,13},{21,17},{25,29}} | collective-permute-start | bytes 1536008 | tf_op jit(solution)/shard_map/ppermute | solution.py:484
  29.5 4.7 %collective-permute-start.8 = (bf16[512,640]{1,0:T(8,128)(2,1)S(1)}, bf16[512,640]{1,0:T(8,128)(2,1)S(1)}, u32[]{:S(2)}, u32[]{:S(2)}) collective-permute-start(bf16[512,640]{1,0:T(8,128)(2,1)S(1)} %get-tuple-element.38), channel_id=1, source_target_pairs={{0,1},{4,5},{8,9},{12,13}} | collective-permute-start | bytes 1966088 | tf_op jit(solution)/shard_map/ppermute | solution.py:484
  30.2 5.4 %collective-permute-start.9 = (bf16[512,640]{1,0:T(8,128)(2,1)S(1)}, bf16[512,640]{1,0:T(8,128)(2,1)S(1)}, u32[]{:S(2)}, u32[]{:S(2)}) collective-permute-start(bf16[512,640]{1,0:T(8,128)(2,1)S(1)} %get-tuple-element.38), channel_id=1, source_target_pairs={{3,19},{7,23},{11,27},{15,31}} | collective-permute-start | bytes 1966088 | tf_op jit(solution)/shard_map/ppermute | solution.py:484
  31.5 4.8 %collective-permute-start.12 = (bf16[400,640]{1,0:T(8,128)(2,1)S(1)}, bf16[400,640]{1,0:T(8,128)(2,1)S(1)}, u32[]{:S(2)}, u32[]{:S(2)}) collective-permute-start(bf16[400,640]{1,0:T(8,128)(2,1)S(1)} %fusion.refs_4_.refs_0_), channel_id=1, source_target_pairs={{23,27},{27,23}} | collective-permute-start | bytes 1536008 | tf_op jit(solution)/shard_map/ppermute | solution.py:484
  32.2 4.1 %collective-permute-start.13 = (bf16[400,640]{1,0:T(8,128)(2,1)S(1)}, bf16[400,640]{1,0:T(8,128)(2,1)S(1)}, u32[]{:S(2)}, u32[]{:S(2)}) collective-permute-start(bf16[400,640]{1,0:T(8,128)(2,1)S(1)} %fusion.refs_4_.refs_0_), channel_id=1, source_target_pairs={{19,23},{23,19},{27,31},{31,27}} | collective-permute-start | bytes 1536008 | tf_op jit(solution)/shard_map/ppermute | solution.py:484
  32.9 3.4 %collective-permute-start.14 = (bf16[400,640]{1,0:T(8,128)(2,1)S(1)}, bf16[400,640]{1,0:T(8,128)(2,1)S(1)}, u32[]{:S(2)}, u32[]{:S(2)}) collective-permute-start(bf16[400,640]{1,0:T(8,128)(2,1)S(1)} %collective-permute-done.11.refs_1_), channel_id=1, source_target_pairs={{23,19},{27,31}} | collective-permute-start | bytes 1536008 | tf_op jit(solution)/shard_map/ppermute | solution.py:484
  34.2 5.4 %collective-permute-start.16 = (bf16[512,640]{1,0:T(8,128)(2,1)S(1)}, bf16[512,640]{1,0:T(8,128)(2,1)S(1)}, u32[]{:S(2)}, u32[]{:S(2)}) collective-permute-start(bf16[512,640]{1,0:T(8,128)(2,1)S(1)} %shard_map.87.sides), channel_id=1, source_target_pairs={{18,17},{22,21},{26,25},{30,29}} | collective-permute-start | bytes 1966088 | tf_op jit(solution)/shard_map/ppermute | solution.py:484
  35.6 4.0 %collective-permute-start.10 = (bf16[256,640]{1,0:T(8,128)(2,1)S(1)}, bf16[256,640]{1,0:T(8,128)(2,1)S(1)}, u32[]{:S(2)}, u32[]{:S(2)}) collective-permute-start(bf16[256,640]{1,0:T(8,128)(2,1)S(1)} %get-tuple-element.43), channel_id=1, source_target_pairs={{1,17},{5,21},{9,25},{13,29}} | collective-permute-start | bytes 983048 | tf_op jit(solution)/shard_map/ppermute | solution.py:484
  36.9 2.7 %collective-permute-start.15 = (bf16[256,640]{1,0:T(8,128)(2,1)S(1)}, bf16[256,640]{1,0:T(8,128)(2,1)S(1)}, u32[]{:S(2)}, u32[]{:S(2)}) collective-permute-start(bf16[256,640]{1,0:T(8,128)(2,1)S(1)} %shard_map.90), channel_id=1, source_target_pairs={{19,17},{23,21},{27,25},{31,29}} | collective-permute-start | bytes 983048 | tf_op jit(solution)/shard_map/ppermute | solution.py:484
  37.6 19.6 %collective-permute-start.18 = (bf16[256,640]{1,0:T(8,128)(2,1)S(1)}, bf16[256,640]{1,0:T(8,128)(2,1)S(1)}, u32[]{:S(2)}, u32[]{:S(2)}) collective-permute-start(bf16[256,640]{1,0:T(8,128)(2,1)S(1)} %get-tuple-element.48.own), channel_id=1, source_target_pairs={{0,2},{4,6},{8,10},{12,14}} | collective-permute-start | bytes 983048 | tf_op jit(solution)/shard_map/ppermute | solution.py:484
  38.9 18.3 %collective-permute-start.19 = (bf16[256,640]{1,0:T(8,128)(2,1)S(1)}, bf16[256,640]{1,0:T(8,128)(2,1)S(1)}, u32[]{:S(2)}, u32[]{:S(2)}) collective-permute-start(bf16[256,640]{1,0:T(8,128)(2,1)S(1)} %get-tuple-element.48.own), channel_id=1, source_target_pairs={{0,3},{4,7},{8,11},{12,15}} | collective-permute-start | bytes 983048 | tf_op jit(solution)/shard_map/ppermute | solution.py:484
  40.2 19.2 %collective-permute-start.17 = (bf16[256,640]{1,0:T(8,128)(2,1)S(1)}, bf16[256,640]{1,0:T(8,128)(2,1)S(1)}, u32[]{:S(2)}, u32[]{:S(2)}) collective-permute-start(bf16[256,640]{1,0:T(8,128)(2,1)S(1)} %get-tuple-element.47), channel_id=1, source_target_pairs={{17,1},{21,5},{25,9},{29,13}} | collective-permute-start | bytes 983048 | tf_op jit(solution)/shard_map/ppermute | solution.py:484
  40.9 18.5 %collective-permute-start.20 = (bf16[256,640]{1,0:T(8,128)(2,1)S(1)}, bf16[256,640]{1,0:T(8,128)(2,1)S(1)}, u32[]{:S(2)}, u32[]{:S(2)}) collective-permute-start(bf16[256,640]{1,0:T(8,128)(2,1)S(1)} %get-tuple-element.51), channel_id=1, source_target_pairs={{0,1},{4,5},{8,9},{12,13}} | collective-permute-start | bytes 983048 | tf_op jit(solution)/shard_map/ppermute | solution.py:484
  60.1 2.7 %collective-permute-start.21 = (bf16[320,640]{1,0:T(8,128)(2,1)S(1)}, bf16[320,640]{1,0:T(8,128)(2,1)S(1)}, u32[]{:S(2)}, u32[]{:S(2)}) collective-permute-start(bf16[320,640]{1,0:T(8,128)(2,1)S(1)} %get-tuple-element.58), channel_id=1, source_target_pairs={{1,0},{5,4},{9,8},{13,12}} | collective-permute-start | bytes 1228808 | tf_op jit(solution)/shard_map/ppermute | solution.py:484
  60.8 2.0 %collective-permute-start.22 = (bf16[320,640]{1,0:T(8,128)(2,1)S(1)}, bf16[320,640]{1,0:T(8,128)(2,1)S(1)}, u32[]{:S(2)}, u32[]{:S(2)}) collective-permute-start(bf16[320,640]{1,0:T(8,128)(2,1)S(1)} %get-tuple-element.57), channel_id=1, source_target_pairs={{1,3},{5,7},{9,11},{13,15}} | collective-permute-start | bytes 1228808 | tf_op jit(solution)/shard_map/ppermute | solution.py:484
  61.5 31.9 %collective-permute-start.23 = (bf16[320,640]{1,0:T(8,128)(2,1)S(1)}, bf16[320,640]{1,0:T(8,128)(2,1)S(1)}, u32[]{:S(2)}, u32[]{:S(2)}) collective-permute-start(bf16[320,640]{1,0:T(8,128)(2,1)S(1)} %get-tuple-element.56), channel_id=1, source_target_pairs={{1,2},{5,6},{9,10},{13,14}} | collective-permute-start | bytes 1228808 | tf_op jit(solution)/shard_map/ppermute | solution.py:484
  94.8 2.5 %collective-permute-start.24 = (bf16[4,56,640]{2,1,0:T(8,128)(2,1)S(1)}, bf16[4,56,640]{2,1,0:T(8,128)(2,1)S(1)}, u32[]{:S(2)}, u32[]{:S(2)}) collective-permute-start(bf16[4,56,640]{2,1,0:T(8,128)(2,1)S(1)} %get-tuple-element.55), channel_id=1, source_target_pairs={{0,16},{1,17},{2,18},{3,19},{4,20},{5,21},{6,22},{7,23},{8,24},{9,... | collective-permute-start | bytes 860168 | tf_op jit(solution)/shard_map/ppermute | solution.py:484
